TPU v7x, 512 devices: a whole 4x4x16 slice. The times are simulated.
512 devices in a mesh: well: 64 (over z_lo, x, core), shot: 8 (over z_hi, y).
Axes of the slice: x: 4, y: 4, z: 16 (z_hi: 2, z_lo: 8; z = z_hi * 8 + z_lo), core: 2. Of those that a mesh axis runs over, the one named last changes fastest.
Arguments:
- traces: bfloat16 [64, 2048, 1024], P('shot', 'well'), may hold values from -6 to 6
- gate_starts: int32 [64, 2048], P('shot'), may hold values from 0 to 896
- section_offsets: int32 [128], P('well'), may hold values from 0 to 240, as said below
Outputs:
- cross_spectra: float32 [2048, 16, 1026], P(('well', 'shot'))
Inputs may be any that keep to these rules, and one draw needn't show every extreme that they name: `section_offsets`: one offset a section; some section has offset 0 and some has 240.
All inputs are finite; a program needn't handle non-finite values.
Results may differ from a plain program's by a relative error of at most 0.007.
Values may be sent and summed in bfloat16 or wider, within the bound.
A program may use at most 64 MiB of HBM per device.

v0:
```python
import math

import jax
import jax.numpy as jnp
from jax import lax
from jax.sharding import PartitionSpec as P

NT = 1024
W = 128
SEC = 16
SPAN = 256
PARTNERS = 16


two_pi = 2.0 * math.pi


def passed_along(value, axis, steps):
    count = lax.axis_size(axis)
    initial, last = (max(0, -steps), min(count, count - steps))
    return lax.ppermute(value, axis, [(source, source + steps) for source in range(initial, last)])


def make_tables():
    sample_steps = jnp.arange(W, dtype=jnp.int32)
    window_taper = 0.5 - 0.5 * jnp.cos((sample_steps.astype(jnp.float32) + 0.5) * (two_pi / W))
    freq_count = NT // 2 + 1
    frequency = jnp.arange(freq_count, dtype=jnp.int32)
    phase_index = sample_steps[:, None] * frequency[None, :] % NT
    phase_angle = phase_index.astype(jnp.float32) * (two_pi / NT)
    scale_factor = 1.0 / math.sqrt(W)
    freq_table = (
        jnp.concatenate([jnp.cos(phase_angle), -jnp.sin(phase_angle)], axis=1) * scale_factor
    ).astype(jnp.bfloat16)
    return (window_taper, freq_table)


def gate_windows(trace_rows, gate_rows, window_taper):
    lead_shape = trace_rows.shape[:-1]
    sample_count = trace_rows.shape[-1]
    flat_rows = trace_rows.reshape(-1, sample_count)
    flat_gates = gate_rows.reshape(-1)
    row_total = flat_rows.shape[0]
    block_size = math.gcd(row_total, 8)
    block_count = row_total // block_size
    blocked_rows = flat_rows.reshape(block_count, block_size, sample_count)
    blocked_gates = flat_gates.reshape(block_count, block_size)
    sample_index = jnp.arange(sample_count, dtype=jnp.int32)
    gate_steps = jnp.arange(W, dtype=jnp.int32)

    def pick_block(inputs):
        rows_here, gates_here = inputs
        selector = (
            sample_index[None, :, None] == gates_here[:, None, None] + gate_steps[None, None, :]
        ).astype(jnp.bfloat16)
        return jnp.einsum("rt,rtu->ru", rows_here, selector, preferred_element_type=jnp.float32)

    picked = lax.map(pick_block, (blocked_rows, blocked_gates))
    picked = picked.reshape(lead_shape + (W,))
    return (window_taper * picked).astype(jnp.bfloat16)


def spectra_of(windows, gate_rows, freq_table):
    lead_shape = windows.shape[:-1]
    freq_count = freq_table.shape[1] // 2
    unrotated = jnp.dot(windows.reshape(-1, W), freq_table, preferred_element_type=jnp.float32)
    unrotated = unrotated.reshape(lead_shape + (2 * freq_count,))
    frequency = jnp.arange(freq_count, dtype=jnp.int32)
    phase_angle = (gate_rows[..., None] * frequency % NT).astype(jnp.float32) * (two_pi / NT)
    cosine = jnp.cos(phase_angle)
    sine_part = jnp.sin(phase_angle)
    real_in = unrotated[..., :freq_count]
    imag_in = unrotated[..., freq_count:]
    rotated = jnp.concatenate(
        [cosine * real_in + sine_part * imag_in, cosine * imag_in - sine_part * real_in], axis=-1
    )
    return rotated.astype(jnp.bfloat16)


def shot_product(left, right):
    return jnp.einsum("srf,srf->rf", left, right, preferred_element_type=jnp.float32)


def section_cross(own_spec, partner_block):
    freq_count = own_spec.shape[-1] // 2
    sec_rows = own_spec.shape[1]
    own_real = own_spec[..., :freq_count]
    own_imag = own_spec[..., freq_count:]
    rows_out = []
    for partner in range(PARTNERS):
        other = partner_block[:, partner : partner + sec_rows]
        other_real = other[..., :freq_count]
        other_imag = other[..., freq_count:]
        real_part = shot_product(own_real, other_real) + shot_product(own_imag, other_imag)
        imag_part = shot_product(own_real, other_imag) - shot_product(own_imag, other_real)
        rows_out.append(jnp.concatenate([real_part, imag_part], axis=-1))
    return jnp.stack(rows_out, axis=1)


def reach_ahead(payload, hop_count):
    pieces = [payload]
    for distance in range(1, hop_count + 1):
        pieces.append(passed_along(payload, "well", -distance))
    extended = jnp.concatenate(pieces, axis=1)
    return extended


def local(traces, gate_starts, section_offsets):
    recv_count = traces.shape[1]
    window_taper, freq_table = make_tables()
    position = lax.axis_index("well")
    hop_count = (recv_count + SPAN - 2) // recv_count
    padded_gates = jnp.pad(gate_starts, ((0, 0), (0, hop_count * recv_count)))
    reach_gates = lax.dynamic_slice_in_dim(
        padded_gates, position * recv_count, (hop_count + 1) * recv_count, 1
    )
    own_gates = reach_gates[:, :recv_count]
    windows = gate_windows(traces, own_gates, window_taper)
    spectra = spectra_of(windows, own_gates, freq_table)
    arrived_windows = reach_ahead(windows, hop_count)
    pieces = [spectra]
    for shard_number in range(1, hop_count + 1):
        first_row = shard_number * recv_count
        pieces.append(
            spectra_of(
                arrived_windows[:, first_row : first_row + recv_count],
                reach_gates[:, first_row : first_row + recv_count],
                freq_table,
            )
        )
    extended = jnp.concatenate(pieces, axis=1)
    results = []
    for section in range(recv_count // SEC):
        offset = section_offsets[section]
        own_spec = spectra[:, section * SEC : (section + 1) * SEC]
        partner_block = lax.dynamic_slice_in_dim(
            extended, section * SEC + offset, SEC + PARTNERS - 1, 1
        )
        results.append(section_cross(own_spec, partner_block))
    pair_terms = jnp.concatenate(results, axis=0)
    return lax.psum_scatter(pair_terms, "shot", scatter_dimension=0, tiled=True)


def solution(mesh):
    in_specs = (P("shot", "well", None), P("shot", None), P("well"))
    out_specs = P(("well", "shot"), None, None)
    return jax.shard_map(local, mesh=mesh, in_specs=in_specs, out_specs=out_specs, check_vma=False)
```

profile of v0, /device:TPU:2, one launch (start us, length us, event | category | flops | bytes accessed | tf_op | source)
XLA Modules:
  0.0 308.5 jit_solution(15495090855876562703)
XLA Ops:
  6.6 1.0 pad_dynamic-slice_fusion.8
  7.6 52.8 %while.11 = (s32[]{:T(128)}, f32[32,8,128]{2,1,0:T(8,128)S(1)}, bf16[32,8,1024]{2,1,0:T(8,128)(2,1)}, s32[32,8]{1,0:T(8,128)S(1)}, s32[]{:T(128)}) while((s32[]{:T(128)}, f32[32,8,128]{2,1,0:T(8,128)S(1)}, bf16[32,8,1024]{2,1,0:T(8,128)(2,1)}, s32[32,8]{1,0:T(8,128)S(1)}, s32[]{:T(128)}) %tuple.236), condition=%wide.region_1.2_spmd.clone, body=%wide.region_0.1_spmd.clone.sunk | while | flops 3146754 | bytes 69801 | solution.py:58
  8.4 0.8 fusion.251
  10.1 0.8 fusion.251
  11.7 0.8 fusion.251
  13.4 0.8 fusion.251
  15.0 0.8 fusion.251
  16.7 0.8 fusion.251
  18.3 0.8 fusion.251
  20.0 0.8 fusion.251
  21.6 0.8 fusion.251
  23.3 0.8 fusion.251
  24.9 0.8 fusion.251
  26.6 0.8 fusion.251
  28.2 0.8 fusion.251
  29.9 0.8 fusion.251
  31.5 0.8 fusion.251
  33.2 0.8 fusion.251
  34.8 0.8 fusion.251
  36.5 0.8 fusion.251
  44.7 0.8 fusion.251
  49.7 0.8 fusion.251
  54.7 0.8 fusion.251
  60.5 1.9 collective-permute-start
  62.4 7.2 %collective-permute-start.1 = (bf16[8,32,128]{2,1,0:T(8,128)(2,1)S(1)}, bf16[8,32,128]{2,1,0:T(8,128)(2,1)S(1)}, u32[]{:S(2)}, u32[]{:S(2)}) collective-permute-start(bf16[8,32,128]{2,1,0:T(8,128)(2,1)S(1)} %fusion.217), channel_id=1, source_target_pairs={{16,0},{24,8},{32,16},{40,24},{48,32},{56,40},{64,48},{72,56},{80,... | collective-permute-start | bytes 196616 | tf_op jit(solution)/shard_map/ppermute | solution.py:21
  69.6 1.3 collective-permute-start.2
  70.9 1.3 collective-permute-start.3
  72.2 1.3 collective-permute-start.4
  73.5 1.0 fusion.216
  74.5 1.0 sine_negate_fusion
  75.9 3.1 %add_convert_fusion.8 = (bf16[8,32,513]{2,1,0:T(8,128)(2,1)S(1)}, bf16[8,32,513]{2,1,0:T(8,128)(2,1)S(1)}) fusion(f32[8,32,1026]{2,1,0:T(8,128)S(1)} %fusion.219, s32[8,32]{1,0:T(8,128)S(1)} %get-tuple-element.275), kind=kLoop, calls=%fused_computation.227 | loop fusion | flops 2889216 | bytes 1576960 | tf_op jit(solution)/shard_map/convert.16
  79.0 1.0 maximum_dynamic-update-slice_fusion.8
  83.7 1.3 collective-permute-start.5
  85.4 1.3 collective-permute-start.6
  87.0 6.2 %add_convert_fusion.6 = (bf16[8,32,513]{2,1,0:T(8,128)(2,1)S(1)}, bf16[8,32,513]{2,1,0:T(8,128)(2,1)S(1)}, bf16[8,32,513]{2,1,0:T(8,128)(2,1)S(1)}, bf16[8,32,513]{2,1,0:T(8,128)(2,1)S(1)}) fusion(f32[8,32,1026]{2,1,0:T(8,128)S(1)} %fusion.221, s32[8,32]{1,0:T(8,128)S(1)} %get-tuple-element.277, f32[8,32,1026]{2,1,0:T(8,128)S(1)} %fusion.220, ...), kind=kLoop, calls=%fused_computation.219 | loop fusion | flops 5778432 | bytes 3153920 | tf_op jit(solution)/shard_map/convert.12
  93.4 1.3 collective-permute-start.7
  95.5 6.2 %add_convert_fusion.4 = (bf16[8,32,513]{2,1,0:T(8,128)(2,1)S(1)}, bf16[8,32,513]{2,1,0:T(8,128)(2,1)S(1)}, bf16[8,32,513]{2,1,0:T(8,128)(2,1)S(1)}, bf16[8,32,513]{2,1,0:T(8,128)(2,1)S(1)}) fusion(f32[8,32,1026]{2,1,0:T(8,128)S(1)} %fusion.223, s32[8,32]{1,0:T(8,128)S(1)} %get-tuple-element.279, f32[8,32,1026]{2,1,0:T(8,128)S(1)} %fusion.222, ...), kind=kLoop, calls=%fused_computation.211 | loop fusion | flops 5778432 | bytes 3153920 | tf_op jit(solution)/shard_map/convert.8
  102.7 6.2 %add_convert_fusion.2 = (bf16[8,32,513]{2,1,0:T(8,128)(2,1)S(1)}, bf16[8,32,513]{2,1,0:T(8,128)(2,1)S(1)}, bf16[8,32,513]{2,1,0:T(8,128)(2,1)S(1)}, bf16[8,32,513]{2,1,0:T(8,128)(2,1)S(1)}) fusion(f32[8,32,1026]{2,1,0:T(8,128)S(1)} %fusion.225, s32[8,32]{1,0:T(8,128)S(1)} %get-tuple-element.281, f32[8,32,1026]{2,1,0:T(8,128)S(1)} %fusion.224, ...), kind=kLoop, calls=%fused_computation.203 | loop fusion | flops 5778432 | bytes 3153920 | tf_op jit(solution)/shard_map/convert.4
  109.9 6.4 %add_convert_fusion = (bf16[8,32,513]{2,1,0:T(8,128)(2,1)S(1)}, bf16[8,32,513]{2,1,0:T(8,128)(2,1)S(1)}, bf16[8,32,513]{2,1,0:T(8,128)(2,1)S(1)}, bf16[8,32,513]{2,1,0:T(8,128)(2,1)S(1)}) fusion(f32[8,32,1026]{2,1,0:T(8,128)S(1)} %fusion.227, s32[8,32]{1,0:T(8,128)S(1)} %get-tuple-element.274, f32[8,32,1026]{2,1,0:T(8,128)S(1)} %fusion.226, ...), kind=kLoop, calls=%fused_computation.195 | loop fusion | flops 5778432 | bytes 3153920 | tf_op jit(solution)/shard_map/convert
  116.6 2.1 fusion.85
  118.7 2.1 fusion.117
  120.8 2.0 fusion.119
  122.8 1.8 fusion.87
  124.6 1.1 fusion.99
  125.7 2.2 fusion.115
  127.9 2.1 fusion.121
  133.8 2.8 copy.5
  136.6 165.0 %reduce-scatter.2.cloned.1.call-done = f32[4,16,1026]{2,1,0:T(8,128)} async-done(((f32[32,16,1026]{2,1,0:T(8,128)}), f32[4,16,1026]{2,1,0:T(8,128)}) %reduce-scatter.2.cloned.1.call-update) | async-done | bytes 262672 | tf_op jit(solution)/shard_map/reduce_scatter | solution.py:141
  (273 shorter events, 43.4 us)
Async XLA Ops:
  6.5 295.1 %reduce-scatter.2.cloned.1.call-start = ((), (), s32[]{:S(2)}) async-start(), calls=%async_computation.1 | async-start | bytes 2654208 | tf_op jit(solution)/shard_map/reduce_scatter | solution.py:141
  60.5 23.3 %collective-permute-start = (bf16[8,32,128]{2,1,0:T(8,128)(2,1)S(1)}, bf16[8,32,128]{2,1,0:T(8,128)(2,1)S(1)}, u32[]{:S(2)}, u32[]{:S(2)}) collective-permute-start(bf16[8,32,128]{2,1,0:T(8,128)(2,1)S(1)} %fusion.217), channel_id=1, source_target_pairs={{8,0},{16,8},{24,16},{32,24},{40,32},{48,40},{56,48},{64,56},{72,6... | collective-permute-start | bytes 196616 | tf_op jit(solution)/shard_map/ppermute | solution.py:21
  62.4 23.0 %collective-permute-start.1 = (bf16[8,32,128]{2,1,0:T(8,128)(2,1)S(1)}, bf16[8,32,128]{2,1,0:T(8,128)(2,1)S(1)}, u32[]{:S(2)}, u32[]{:S(2)}) collective-permute-start(bf16[8,32,128]{2,1,0:T(8,128)(2,1)S(1)} %fusion.217), channel_id=1, source_target_pairs={{16,0},{24,8},{32,16},{40,24},{48,32},{56,40},{64,48},{72,56},{80,... | collective-permute-start | bytes 196616 | tf_op jit(solution)/shard_map/ppermute | solution.py:21
  69.6 23.8 %collective-permute-start.2 = (bf16[8,32,128]{2,1,0:T(8,128)(2,1)S(1)}, bf16[8,32,128]{2,1,0:T(8,128)(2,1)S(1)}, u32[]{:S(2)}, u32[]{:S(2)}) collective-permute-start(bf16[8,32,128]{2,1,0:T(8,128)(2,1)S(1)} %fusion.217), channel_id=1, source_target_pairs={{24,0},{32,8},{40,16},{48,24},{56,32},{64,40},{72,48},{80,56},{88,... | collective-permute-start | bytes 196616 | tf_op jit(solution)/shard_map/ppermute | solution.py:21
  70.9 24.3 %collective-permute-start.3 = (bf16[8,32,128]{2,1,0:T(8,128)(2,1)S(1)}, bf16[8,32,128]{2,1,0:T(8,128)(2,1)S(1)}, u32[]{:S(2)}, u32[]{:S(2)}) collective-permute-start(bf16[8,32,128]{2,1,0:T(8,128)(2,1)S(1)} %fusion.217), channel_id=1, source_target_pairs={{32,0},{40,8},{48,16},{56,24},{64,32},{72,40},{80,48},{88,56},{96,... | collective-permute-start | bytes 196616 | tf_op jit(solution)/shard_map/ppermute | solution.py:21
  72.2 29.7 %collective-permute-start.4 = (bf16[8,32,128]{2,1,0:T(8,128)(2,1)S(1)}, bf16[8,32,128]{2,1,0:T(8,128)(2,1)S(1)}, u32[]{:S(2)}, u32[]{:S(2)}) collective-permute-start(bf16[8,32,128]{2,1,0:T(8,128)(2,1)S(1)} %fusion.217), channel_id=1, source_target_pairs={{40,0},{48,8},{56,16},{64,24},{72,32},{80,40},{88,48},{96,56},{104... | collective-permute-start | bytes 196616 | tf_op jit(solution)/shard_map/ppermute | solution.py:21
  75.9 4.1 %copy-start.1 = (s32[2]{0:T(128)S(1)}, s32[2]{0:T(128)}, u32[]{:S(2)}) copy-start(s32[2]{0:T(128)} %param.7) | copy-start | bytes 28
  83.7 18.6 %collective-permute-start.5 = (bf16[8,32,128]{2,1,0:T(8,128)(2,1)S(1)}, bf16[8,32,128]{2,1,0:T(8,128)(2,1)S(1)}, u32[]{:S(2)}, u32[]{:S(2)}) collective-permute-start(bf16[8,32,128]{2,1,0:T(8,128)(2,1)S(1)} %fusion.217), channel_id=1, source_target_pairs={{48,0},{56,8},{64,16},{72,24},{80,32},{88,40},{96,48},{104,56},{11... | collective-permute-start | bytes 196616 | tf_op jit(solution)/shard_map/ppermute | solution.py:21
  85.4 23.7 %collective-permute-start.6 = (bf16[8,32,128]{2,1,0:T(8,128)(2,1)S(1)}, bf16[8,32,128]{2,1,0:T(8,128)(2,1)S(1)}, u32[]{:S(2)}, u32[]{:S(2)}) collective-permute-start(bf16[8,32,128]{2,1,0:T(8,128)(2,1)S(1)} %fusion.217), channel_id=1, source_target_pairs={{56,0},{64,8},{72,16},{80,24},{88,32},{96,40},{104,48},{112,56},{1... | collective-permute-start | bytes 196616 | tf_op jit(solution)/shard_map/ppermute | solution.py:21
  86.7 6.5 %copy-start = (bf16[8,288,1026]{2,1,0:T(8,128)(2,1)S(1)}, bf16[8,288,1026]{2,1,0:T(8,128)(2,1)}, u32[]{:S(2)}) copy-start(bf16[8,288,1026]{2,1,0:T(8,128)(2,1)} %maximum_dynamic-update-slice_fusion.8) | copy-start | bytes 14183428
  93.4 16.2 %collective-permute-start.7 = (bf16[8,32,128]{2,1,0:T(8,128)(2,1)S(1)}, bf16[8,32,128]{2,1,0:T(8,128)(2,1)S(1)}, u32[]{:S(2)}, u32[]{:S(2)}) collective-permute-start(bf16[8,32,128]{2,1,0:T(8,128)(2,1)S(1)} %fusion.217), channel_id=1, source_target_pairs={{64,0},{72,8},{80,16},{88,24},{96,32},{104,40},{112,48},{120,56},{... | collective-permute-start | bytes 196616 | tf_op jit(solution)/shard_map/ppermute | solution.py:21
Sparse Core Ops, SparseCore 0:
  136.8 164.8 reduce-scatter.1
where the time goes:
time: 312 us; the launch traced here: 308 us
  waiting for transfers between devices  165 us (53%)
  other arithmetic  51.5 us (17%)
  matrix products  29.8 us (10%)
  local copies, waits for them, and re-layouts  27.8 us (9%)
  between operations  17.3 us (6%)
  starting transfers between devices  16.9 us (5%)
    reduce_scatter x1, waiting for transfers between devices, local(): return lax.psum_scatter(pair_terms, 'shot', scatter_dimension=0, tiled=True)  165 us
    another operation x5, other arithmetic  28 us
    dot_general x32, matrix products, pick_block(): jnp.einsum('rt,rtu->ru', rows_here, selector, preferred_element_type=jnp....  26.9 us
    squeeze x32, local copies, waits for them, and re-layouts, gate_windows(): picked = lax.map(pick_block, (blocked_rows, blocked_gates))  23.1 us
    ppermute x8, starting transfers between devices, passed_along(): lax.ppermute(value, axis, [(source, source + steps) for source in range(i...  16.9 us
    dot_general x7, other arithmetic, shot_product(): jnp.einsum('srf,srf->rf', left, right, preferred_element_type=jnp.float32)  13.4 us
  transfers between devices with their start and end apart: 9, of which 1 were waited for; matrix products, arithmetic and copies ran while one was open for 9% of the time, Pallas kernels for 0%

commit v1 on v0

v1 whole, which is shorter than its diff:
```python
import functools
import math

import jax
import jax.numpy as jnp
import ml_dtypes
import numpy as np
from jax import lax
from jax.experimental import pallas as pl
from jax.experimental.pallas import tpu as pltpu
from jax.sharding import PartitionSpec as P

NT = 1024
W = 128
SEC = 16
PARTNERS = 16
PLANE = 8
RECV = 32
OWN_PAIRS = 2
REACH_PAIRS = 10
BLOCKS = REACH_PAIRS + OWN_PAIRS + 1
SLOTS = 2 * (REACH_PAIRS + OWN_PAIRS)
MESH = pl.DeviceIdType.MESH
f32 = jnp.float32
bf16 = jnp.bfloat16

SHOT_PEERS = [(1, 0), (1, 1), (1, 3), (1, 2), (0, 1), (0, 3), (0, 2)]


def packed_table():
    steps = np.arange(W)
    k = np.arange(NT // 2)
    angle = ((steps[:, None] * k[None, :]) % NT).astype(np.float32) * np.float32(2 * math.pi / NT)
    real = np.cos(angle)
    imag = -np.sin(angle)
    imag[:, 0] = np.cos(math.pi * steps)
    scale = np.float32(1.0 / math.sqrt(W))
    return (np.concatenate([real, imag], axis=1) * scale).astype(ml_dtypes.bfloat16)


def place():
    well = lax.axis_index("well")
    shot = lax.axis_index("shot")
    return well // PLANE, well % PLANE, shot // 4, shot % 4


def gather_kernel(
    off_ref, traces_hbm, gates_hbm, out_hbm,
    traces, gates, gate_cols, rows, reach, sending,
    load_sem, x_send, x_recv, z_send, z_recv, c_send, c_recv, s_send, s_recv,
):
    z, wp, zh, y = place()
    x, core = wp // 2, wp % 2
    well = z * PLANE + wp
    shot = zh * 4 + y

    def well_at(plane, column, which):
        return plane * PLANE + column * 2 + which

    x_peers = [(x + d) % 4 for d in (1, 3, 2)]
    other_core = (well_at(z, x, 1 - core), shot)
    shot_peers = [((zh + a) % 2 * 4 + (y + b) % 4) for a, b in SHOT_PEERS]

    barrier = pltpu.get_barrier_semaphore()
    for peer in shot_peers:
        pl.semaphore_signal(barrier, inc=1, device_id=(well, peer), device_id_type=MESH)
    for column in x_peers:
        pl.semaphore_signal(barrier, inc=1, device_id=(well_at(z, column, core), shot), device_id_type=MESH)
    pl.semaphore_signal(barrier, inc=1, device_id=other_core, device_id_type=MESH)

    @pl.when(z < 7)
    def _():
        for column in range(4):
            pl.semaphore_signal(barrier, inc=1, device_id=(well_at(z + 1, column, core), shot), device_id_type=MESH)

    load_traces = pltpu.make_async_copy(traces_hbm, traces, load_sem.at[0])
    load_traces.start()
    here = pl.multiple_of(z * 256, 256)
    ahead = pl.multiple_of(jnp.minimum(z + 1, 7) * 256, 256)
    load_here = pltpu.make_async_copy(gates_hbm.at[:, pl.ds(here, 256)], gates.at[:, pl.ds(0, 256)], load_sem.at[1])
    load_ahead = pltpu.make_async_copy(gates_hbm.at[:, pl.ds(ahead, 256)], gates.at[:, pl.ds(256, 256)], load_sem.at[2])
    load_here.start()
    load_ahead.start()

    @pl.when(z == 7)
    def _():
        reach[pl.ds(128, 128)] = jnp.zeros((128, 16, W), bf16)

    load_here.wait()
    load_ahead.wait()
    all_gates = gates[...]
    gate_cols[...] = jnp.transpose(all_gates[:, :256].astype(f32))
    lane = lax.broadcasted_iota(jnp.int32, (RECV, W), 1)
    taper = 0.5 - 0.5 * jnp.cos((lane[:8].astype(f32) + 0.5) * (2 * math.pi / W))
    taper = jnp.concatenate([taper] * (RECV // 8), axis=0)
    columns = gate_cols[pl.ds(pl.multiple_of(wp * RECV, RECV), RECV), :].astype(jnp.int32)
    load_traces.wait()
    for s in range(8):
        data = traces[s].astype(f32)
        gate = jnp.broadcast_to(columns[:, s : s + 1], (RECV, W))
        fine = gate & 127
        tiles = [data[:, k * W : (k + 1) * W] for k in range(8)]
        pick = (gate & 512) != 0
        four = [jnp.where(pick, tiles[k + 4], tiles[k]) for k in range(4)] + [tiles[4]]
        pick = (gate & 256) != 0
        three = [jnp.where(pick, four[k + 2], four[k]) for k in range(3)]
        pick = (gate & 128) != 0
        low = jnp.where(pick, three[1], three[0])
        high = jnp.where(pick, three[2], three[1])
        turned = jnp.where(lane >= fine, low, high)
        for bit in range(7):
            step = 1 << bit
            turned = jnp.where((fine & step) != 0, pltpu.roll(turned, W - step, 1), turned)
        rows[pl.ds(s, RECV, stride=8), :] = turned * taper
    own_first = pl.multiple_of(wp * 16, 16)
    reach[pl.ds(own_first, 16)] = rows[...].reshape(16, 16, W).astype(bf16)

    halves = jnp.concatenate([all_gates >> 3, all_gates & 7], axis=0).astype(f32).astype(bf16)
    lanes = lax.broadcasted_iota(jnp.int32, (512, W), 1)
    index = lax.broadcasted_iota(jnp.int32, (512, W), 0)
    members = [(a, b) for a, b in SHOT_PEERS] + [(0, 0)]
    for k, (a, b) in enumerate(members):
        to_zh, to_y = (zh + a) % 2, (y + b) % 4
        own = wp * RECV + to_zh * SEC + to_y * 4
        start = (own + off_ref[to_zh]) // 2 * 2
        wanted = jnp.where(lanes < 32, start + lanes, own - 32 + lanes)
        chosen = jnp.where(index == wanted, 1.0, 0.0).astype(bf16)
        block = jnp.dot(halves, chosen, preferred_element_type=f32)
        sending[k, BLOCKS - 1] = block.astype(bf16)

    @pl.when(z > 0)
    def _():
        pl.semaphore_wait(barrier, 15)

    @pl.when(z == 0)
    def _():
        pl.semaphore_wait(barrier, 11)

    def slot(plane, column, which):
        first = pl.multiple_of((plane * PLANE + column * 2 + which) * 16, 16)
        return reach.at[pl.ds(first, 16)]

    mine = slot(0, x, core)
    x_copies = []
    for i, column in enumerate(x_peers):
        copy = pltpu.make_async_remote_copy(
            src_ref=mine, dst_ref=mine, send_sem=x_send.at[i], recv_sem=x_recv.at[i],
            device_id=(well_at(z, column, core), shot), device_id_type=MESH,
        )
        copy.start()
        x_copies.append(copy)

    def z_copy(i):
        return pltpu.make_async_remote_copy(
            src_ref=mine, dst_ref=slot(1, x, core), send_sem=z_send.at[i], recv_sem=z_recv.at[i],
            device_id=(well_at(jnp.maximum(z - 1, 0), (x + i) % 4, core), shot), device_id_type=MESH,
        )

    @pl.when(z > 0)
    def _():
        for i in range(4):
            z_copy(i).start()

    def c_copy(plane, column, i):
        block = slot(plane, column, core)
        return pltpu.make_async_remote_copy(
            src_ref=block, dst_ref=block, send_sem=c_send.at[i], recv_sem=c_recv.at[i],
            device_id=other_core, device_id_type=MESH,
        )

    c_copies = [c_copy(0, x, 0)]
    c_copies[0].start()
    for i, d in enumerate((1, 3, 2)):
        x_copies[i].wait_recv()
        copy = c_copy(0, (x - d + 4) % 4, 1 + i)
        copy.start()
        c_copies.append(copy)

    @pl.when(z < 7)
    def _():
        for i in range(4):
            z_copy(i).wait_recv()
            c_copy(1, (x - i + 4) % 4, 4 + i).start()

    for i in range(4):
        c_copies[i].wait()

    @pl.when(z < 7)
    def _():
        for i in range(4):
            c_copy(1, (x - i + 4) % 4, 4 + i).wait()

    s_copies = []
    for k, (a, b) in enumerate(members):
        to_zh, to_y = (zh + a) % 2, (y + b) % 4
        own = wp * 16 + to_zh * 8 + to_y * 2
        first = own + off_ref[to_zh] // 2
        sending[k, :REACH_PAIRS] = reach[pl.ds(first, REACH_PAIRS)]
        sending[k, REACH_PAIRS : REACH_PAIRS + OWN_PAIRS] = reach[pl.ds(own, OWN_PAIRS)]
        if k < 7:
            copy = pltpu.make_async_remote_copy(
                src_ref=sending.at[k], dst_ref=out_hbm.at[shot], send_sem=s_send.at[k], recv_sem=s_recv.at[k],
                device_id=(well, shot_peers[k]), device_id_type=MESH,
            )
        else:
            copy = pltpu.make_async_copy(sending.at[k], out_hbm.at[shot], load_sem.at[3])
        copy.start()
        s_copies.append(copy)
    for copy in x_copies:
        copy.wait_send()

    @pl.when(z > 0)
    def _():
        for i in range(4):
            z_copy(i).wait_send()

    for copy in s_copies:
        copy.wait()


def turn(angle):
    half = angle * math.pi
    sq = half * half
    sine = half * (1.0 + sq * (-1 / 6 + sq * (1 / 120 + sq * (-1 / 5040 + sq * (1 / 362880 - sq * (1 / 39916800))))))
    cosine = 1.0 + sq * (
        -0.5 + sq * (1 / 24 + sq * (-1 / 720 + sq * (1 / 40320 + sq * (-1 / 3628800 + sq * (1 / 479001600)))))
    )
    return 1.0 - 2.0 * sine * sine, 2.0 * sine * cosine


def fraction(value):
    return value - jnp.round(value)


def fold(parts):
    row = lax.broadcasted_iota(jnp.int32, (8, W), 0)
    while len(parts) > 1:
        half = len(parts) // 2
        upper = (row & half) == 0
        merged = []
        for i in range(half):
            first, second = parts[i], parts[i + half]
            kept = jnp.where(upper, first, second)
            moved = jnp.where(upper, second, first)
            if half == 4:
                moved = pltpu.roll(moved, 4, 0)
            else:
                moved = jnp.where(upper, pltpu.roll(moved, 8 - half, 0), pltpu.roll(moved, half, 0))
            merged.append(kept + moved)
        parts = merged
    return parts[0]


def cross_kernel(off_ref, data, table, out, flat, gate_vals, spectra):
    z, wp, zh, y = place()
    odd = off_ref[zh] & 1
    lane = lax.broadcasted_iota(jnp.int32, (8, W), 1)
    lane_f = lane.astype(f32)

    for k in range(8):
        block = data[k, BLOCKS - 1].astype(f32)
        gate = block[:8] * 8.0 + block[8:]
        step_cos, step_sin = turn(fraction(gate * 0.125))
        for slot in range(SLOTS):
            column = slot if slot < 20 else 12 + slot
            for i, value in enumerate((gate, step_cos, step_sin)):
                gate_vals[slot, k, i] = jnp.broadcast_to(value[:, column : column + 1], (8, W))

    @pl.loop(0, SLOTS // 2)
    def _(p):
        left = data[:, p].reshape(8 * 16, W)
        flat[...] = jnp.dot(left, table[...], preferred_element_type=f32)
        for par in range(2):
            slot = 2 * p + par
            for k in range(8):
                first = k * 16 + par * 8
                gate = gate_vals[slot, k, 0]
                step_cos = gate_vals[slot, k, 1]
                step_sin = gate_vals[slot, k, 2]
                cosine, sine = turn(fraction(gate * (lane_f * (1.0 / NT))))
                for t in range(4):
                    real = flat[first : first + 8, t * W : (t + 1) * W]
                    imag = flat[first : first + 8, (4 + t) * W : (5 + t) * W]
                    if t == 0:
                        alternating = 1.0 - 2.0 * jnp.abs(gate - 2.0 * jnp.floor(gate * 0.5))
                        imag_cos = jnp.where(lane == 0, alternating, cosine)
                    else:
                        imag_cos = cosine
                    new_real = cosine * real + sine * imag
                    new_imag = imag_cos * imag - sine * real
                    rows = slice(k * 8, k * 8 + 8)
                    spectra[slot, t, 0, rows, :] = new_real.astype(bf16).astype(f32)
                    spectra[slot, t, 1, rows, :] = new_imag.astype(bf16).astype(f32)
                    if t < 3:
                        cosine, sine = (
                            cosine * step_cos - sine * step_sin,
                            sine * step_cos + cosine * step_sin,
                        )

    @pl.loop(0, 4)
    def _(a):
        imags = []
        for t in range(4):
            own = [(spectra[20 + a, t, 0, k * 8 : k * 8 + 8, :], spectra[20 + a, t, 1, k * 8 : k * 8 + 8, :]) for k in range(8)]
            for group in range(2):
                sums = []
                for j in range(8):
                    slot = a + odd + group * 8 + j
                    one = two = three = None
                    for k in range(8):
                        re = spectra[slot, t, 0, k * 8 : k * 8 + 8, :]
                        im = spectra[slot, t, 1, k * 8 : k * 8 + 8, :]
                        first = own[k][0] * re
                        second = own[k][1] * im
                        third = own[k][0] * im - own[k][1] * re
                        one = first if one is None else one + first
                        two = second if two is None else two + second
                        three = third if three is None else three + third
                    sums.append((one, two, three))
                rows = pl.ds(group * 8, 8)
                if t == 0:
                    ones = fold([s[0] for s in sums])
                    twos = fold([s[1] for s in sums])
                    threes = fold([s[2] for s in sums])
                    out[a, rows, :W] = jnp.where(lane == 0, ones, ones + twos)
                    imags.append((twos, jnp.where(lane == 0, 0.0, threes)))
                else:
                    out[a, rows, t * W : (t + 1) * W] = fold([s[0] + s[1] for s in sums])
                    threes = fold([s[2] for s in sums])
                    imags.append((None, threes))
        for group in range(2):
            rows = pl.ds(group * 8, 8)
            before = imags[group][0]
            for t in range(4):
                turned = pltpu.roll(imags[2 * t + group][1], 1, 1)
                out[a, rows, (4 + t) * W : (5 + t) * W] = jnp.where(lane == 0, before, turned)
                before = turned
            out[a, rows, 8 * W : 8 * W + 2] = jnp.where(lane == 0, before, 0.0)[:, :2]


def local(traces, gate_starts, section_offsets):
    any_space = pl.BlockSpec(memory_space=pl.ANY)
    smem = pl.BlockSpec(memory_space=pltpu.SMEM)
    vmem = pl.BlockSpec(memory_space=pltpu.VMEM)
    dma = pltpu.SemaphoreType.DMA
    arrived = pl.pallas_call(
        gather_kernel,
        out_shape=jax.ShapeDtypeStruct((8, BLOCKS, 16, W), bf16),
        in_specs=[smem, any_space, any_space],
        out_specs=any_space,
        scratch_shapes=[
            pltpu.VMEM((8, RECV, NT), bf16),
            pltpu.VMEM((8, 512), jnp.int32),
            pltpu.VMEM((256, 8), f32),
            pltpu.VMEM((RECV * 8, W), f32),
            pltpu.VMEM((256, 16, W), bf16),
            pltpu.VMEM((8, BLOCKS, 16, W), bf16),
            dma((4,)), dma((3,)), dma((3,)), dma((4,)), dma((4,)), dma((8,)), dma((8,)), dma((7,)), dma((7,)),
        ],
        compiler_params=pltpu.CompilerParams(
            collective_id=0, has_side_effects=True, vmem_limit_bytes=16 * 2**20
        ),
        name="gather",
    )(section_offsets, traces, gate_starts)
    return pl.pallas_call(
        cross_kernel,
        out_shape=jax.ShapeDtypeStruct((4, PARTNERS, NT + 2), f32),
        in_specs=[smem, vmem, vmem],
        out_specs=vmem,
        scratch_shapes=[
            pltpu.VMEM((128, NT), f32),
            pltpu.VMEM((SLOTS, 8, 3, 8, W), f32),
            pltpu.VMEM((SLOTS, 4, 2, 64, W), f32),
        ],
        compiler_params=pltpu.CompilerParams(vmem_limit_bytes=32 * 2**20),
        name="cross",
    )(section_offsets, arrived, jnp.asarray(packed_table()))


def solution(mesh):
    in_specs = (P("shot", "well", None), P("shot", None), P("well"))
    out_specs = P(("well", "shot"), None, None)
    return jax.shard_map(local, mesh=mesh, in_specs=in_specs, out_specs=out_specs, check_vma=False)
```

time: 312 us -> 60 us (0.19)
  the two profiles are of different devices: /device:TPU:2 before, /device:TPU:32 now
where the time goes in v1:
time: 60 us; the launch traced here: 59.8 us
  Pallas kernels  57.3 us (96%)
  local copies, waits for them, and re-layouts  2.54 us (4%)
    pallas_call x1, Pallas kernels, local(): pl.pallas_call(gather_kernel, out_shape=jax.ShapeDtypeStruct((8, BLOCKS,...  49 us
    pallas_call x1, Pallas kernels, local(): pl.pallas_call(cross_kernel, out_shape=jax.ShapeDtypeStruct((4, PARTNERS,...  8.24 us
    unnamed x10, local copies, waits for them, and re-layouts  2.54 us

profile of v1, /device:TPU:32, one launch (start us, length us, event | category | flops | bytes accessed | tf_op | source)
XLA Modules:
  0.0 59.8 jit_solution(9330279281737585513)
XLA Ops:
  0.0 0.0 copy-start
  0.0 1.0 %copy-done = bf16[8,32,1024]{2,1,0:T(8,128)(2,1)S(1)} copy-done((bf16[8,32,1024]{2,1,0:T(8,128)(2,1)S(1)}, bf16[8,32,1024]{2,1,0:T(8,128)(2,1)}, u32[]{:S(2)}) %copy-start) | copy-done | bytes 524312
  1.0 0.0 copy-start.2
  1.0 0.8 %copy-done.2 = s32[8,2048]{1,0:T(8,128)S(1)} copy-done((s32[8,2048]{1,0:T(8,128)S(1)}, s32[8,2048]{1,0:T(8,128)}, u32[]{:S(2)}) %copy-start.2) | copy-done | bytes 65560
  1.9 0.0 copy-start.3
  1.9 0.7 %copy-done.3 = s32[2]{0:T(128)S(1)} copy-done((s32[2]{0:T(128)S(1)}, s32[2]{0:T(128)}, u32[]{:S(2)}) %copy-start.3) | copy-done | bytes 32
  2.5 0.0 copy-start.1
  2.5 0.0 copy-start.4
  2.5 49.0 %gather.1.data = bf16[8,13,16,128]{3,2,1,0:T(8,128)(2,1)S(1)} custom-call(s32[2]{0:T(128)S(1)} %copy-done.3, bf16[8,32,1024]{2,1,0:T(8,128)(2,1)S(1)} %copy-done, s32[8,2048]{1,0:T(8,128)S(1)} %copy-done.2), custom_call_target="tpu_custom_call" | custom-call | tf_op jit(solution)/shard_map/gather/pallas_call | solution.py:346
  51.6 0.0 copy-done.1
  51.6 0.0 copy-done.4
  51.6 8.2 %cross.1 = f32[4,16,1026]{2,1,0:T(8,128)} custom-call(s32[2]{0:T(128)S(1)} %copy-done.4, bf16[8,13,16,128]{3,2,1,0:T(8,128)(2,1)S(1)} %gather.1.data, bf16[128,1024]{1,0:T(8,128)(2,1)S(1)} %copy-done.1), custom_call_target="tpu_custom_call" | custom-call | tf_op jit(solution)/shard_map/cross/pallas_call | solution.py:365
Async XLA Ops:
  0.0 1.0 %copy-start = (bf16[8,32,1024]{2,1,0:T(8,128)(2,1)S(1)}, bf16[8,32,1024]{2,1,0:T(8,128)(2,1)}, u32[]{:S(2)}) copy-start(bf16[8,32,1024]{2,1,0:T(8,128)(2,1)} %traces_hbm.1) | copy-start | bytes 1572868
  1.0 0.8 %copy-start.2 = (s32[8,2048]{1,0:T(8,128)S(1)}, s32[8,2048]{1,0:T(8,128)}, u32[]{:S(2)}) copy-start(s32[8,2048]{1,0:T(8,128)} %gates_hbm.1) | copy-start | bytes 196612
  1.9 0.7 %copy-start.3 = (s32[2]{0:T(128)S(1)}, s32[2]{0:T(128)}, u32[]{:S(2)}) copy-start(s32[2]{0:T(128)} %off_ref.3) | copy-start | bytes 28
  2.5 49.0 %copy-start.1 = (bf16[128,1024]{1,0:T(8,128)(2,1)S(1)}, bf16[128,1024]{1,0:T(8,128)(2,1)}, u32[]{:S(2)}) copy-start(bf16[128,1024]{1,0:T(8,128)(2,1)} %constant.2.clone.table) | copy-start | bytes 786436
  2.5 49.0 %copy-start.4 = (s32[2]{0:T(128)S(1)}, s32[2]{0:T(128)}, u32[]{:S(2)}) copy-start(s32[2]{0:T(128)} %off_ref.3) | copy-start | bytes 28

commit v2 on v1

--- a/solution.py
+++ b/solution.py
@@ -19,13 +19,13 @@
 OWN_PAIRS = 2
 REACH_PAIRS = 10
 BLOCKS = REACH_PAIRS + OWN_PAIRS + 1
+SEC_REACH = 16
+SEC_OWN = 8
+SEC_BLOCKS = SEC_REACH + SEC_OWN + 1
 SLOTS = 2 * (REACH_PAIRS + OWN_PAIRS)
 MESH = pl.DeviceIdType.MESH
 f32 = jnp.float32
 bf16 = jnp.bfloat16
-
-SHOT_PEERS = [(1, 0), (1, 1), (1, 3), (1, 2), (0, 1), (0, 3), (0, 2)]
-
 
 def packed_table():
     steps = np.arange(W)
@@ -45,57 +45,63 @@
 
 
 def gather_kernel(
-    off_ref, traces_hbm, gates_hbm, out_hbm,
-    traces, gates, gate_cols, rows, reach, sending,
-    load_sem, x_send, x_recv, z_send, z_recv, c_send, c_recv, s_send, s_recv,
+    off_hbm, traces_hbm, gates_hbm, out_hbm,
+    off_ref, traces, gates, gate_cols, rows, reach, chosen, far,
+    load_sem, trace_sem, x_send, x_recv, z_send, z_recv, c_send, c_recv,
+    far_send, far_recv, y_send, y_recv, keep_sem,
 ):
     z, wp, zh, y = place()
     x, core = wp // 2, wp % 2
     well = z * PLANE + wp
     shot = zh * 4 + y
+    far_shot = (1 - zh) * 4 + y
 
     def well_at(plane, column, which):
         return plane * PLANE + column * 2 + which
 
     x_peers = [(x + d) % 4 for d in (1, 3, 2)]
+    y_peers = [(y + d) % 4 for d in (1, 3, 2)]
     other_core = (well_at(z, x, 1 - core), shot)
-    shot_peers = [((zh + a) % 2 * 4 + (y + b) % 4) for a, b in SHOT_PEERS]
+    across = (well, far_shot)
 
     barrier = pltpu.get_barrier_semaphore()
-    for peer in shot_peers:
-        pl.semaphore_signal(barrier, inc=1, device_id=(well, peer), device_id_type=MESH)
+    pl.semaphore_signal(barrier, inc=1, device_id=across, device_id_type=MESH)
     for column in x_peers:
         pl.semaphore_signal(barrier, inc=1, device_id=(well_at(z, column, core), shot), device_id_type=MESH)
-    pl.semaphore_signal(barrier, inc=1, device_id=other_core, device_id_type=MESH)
 
     @pl.when(z < 7)
     def _():
         for column in range(4):
             pl.semaphore_signal(barrier, inc=1, device_id=(well_at(z + 1, column, core), shot), device_id_type=MESH)
 
-    load_traces = pltpu.make_async_copy(traces_hbm, traces, load_sem.at[0])
-    load_traces.start()
+    for peer in y_peers:
+        pl.semaphore_signal(barrier, inc=1, device_id=(well, zh * 4 + peer), device_id_type=MESH)
+    pl.semaphore_signal(barrier, inc=1, device_id=other_core, device_id_type=MESH)
+
     here = pl.multiple_of(z * 256, 256)
     ahead = pl.multiple_of(jnp.minimum(z + 1, 7) * 256, 256)
-    load_here = pltpu.make_async_copy(gates_hbm.at[:, pl.ds(here, 256)], gates.at[:, pl.ds(0, 256)], load_sem.at[1])
-    load_ahead = pltpu.make_async_copy(gates_hbm.at[:, pl.ds(ahead, 256)], gates.at[:, pl.ds(256, 256)], load_sem.at[2])
+    load_here = pltpu.make_async_copy(gates_hbm.at[:, pl.ds(here, 256)], gates.at[:, pl.ds(0, 256)], load_sem.at[0])
+    load_ahead = pltpu.make_async_copy(gates_hbm.at[:, pl.ds(ahead, 256)], gates.at[:, pl.ds(256, 256)], load_sem.at[1])
+    load_off = pltpu.make_async_copy(off_hbm, off_ref, load_sem.at[2])
     load_here.start()
+    load_traces = [pltpu.make_async_copy(traces_hbm.at[s], traces.at[s], trace_sem.at[s]) for s in range(8)]
+    for copy in load_traces:
+        copy.start()
     load_ahead.start()
+    load_off.start()
 
     @pl.when(z == 7)
     def _():
         reach[pl.ds(128, 128)] = jnp.zeros((128, 16, W), bf16)
 
-    load_here.wait()
-    load_ahead.wait()
-    all_gates = gates[...]
-    gate_cols[...] = jnp.transpose(all_gates[:, :256].astype(f32))
     lane = lax.broadcasted_iota(jnp.int32, (RECV, W), 1)
     taper = 0.5 - 0.5 * jnp.cos((lane[:8].astype(f32) + 0.5) * (2 * math.pi / W))
     taper = jnp.concatenate([taper] * (RECV // 8), axis=0)
+    load_here.wait()
+    gate_cols[...] = jnp.transpose(gates[:, :256].astype(f32))
     columns = gate_cols[pl.ds(pl.multiple_of(wp * RECV, RECV), RECV), :].astype(jnp.int32)
-    load_traces.wait()
     for s in range(8):
+        load_traces[s].wait()
         data = traces[s].astype(f32)
         gate = jnp.broadcast_to(columns[:, s : s + 1], (RECV, W))
         fine = gate & 127
@@ -115,26 +121,13 @@
     own_first = pl.multiple_of(wp * 16, 16)
     reach[pl.ds(own_first, 16)] = rows[...].reshape(16, 16, W).astype(bf16)
 
-    halves = jnp.concatenate([all_gates >> 3, all_gates & 7], axis=0).astype(f32).astype(bf16)
-    lanes = lax.broadcasted_iota(jnp.int32, (512, W), 1)
-    index = lax.broadcasted_iota(jnp.int32, (512, W), 0)
-    members = [(a, b) for a, b in SHOT_PEERS] + [(0, 0)]
-    for k, (a, b) in enumerate(members):
-        to_zh, to_y = (zh + a) % 2, (y + b) % 4
-        own = wp * RECV + to_zh * SEC + to_y * 4
-        start = (own + off_ref[to_zh]) // 2 * 2
-        wanted = jnp.where(lanes < 32, start + lanes, own - 32 + lanes)
-        chosen = jnp.where(index == wanted, 1.0, 0.0).astype(bf16)
-        block = jnp.dot(halves, chosen, preferred_element_type=f32)
-        sending[k, BLOCKS - 1] = block.astype(bf16)
-
     @pl.when(z > 0)
     def _():
-        pl.semaphore_wait(barrier, 15)
+        pl.semaphore_wait(barrier, 12)
 
     @pl.when(z == 0)
     def _():
-        pl.semaphore_wait(barrier, 11)
+        pl.semaphore_wait(barrier, 8)
 
     def slot(plane, column, which):
         first = pl.multiple_of((plane * PLANE + column * 2 + which) * 16, 16)
@@ -170,6 +163,31 @@
 
     c_copies = [c_copy(0, x, 0)]
     c_copies[0].start()
+
+    load_ahead.wait()
+    load_off.wait()
+    all_gates = gates[...]
+    halves = jnp.concatenate([all_gates >> 3, all_gates & 7], axis=0).astype(f32).astype(bf16)
+    lanes = lax.broadcasted_iota(jnp.int32, (512, W), 1)
+    index = lax.broadcasted_iota(jnp.int32, (512, W), 0)
+    for h in (1, 0):
+        own = wp * RECV + (zh + h) % 2 * SEC
+        start = (own + off_ref[(zh + h) % 2]) // 2 * 2
+        wanted = jnp.where(lanes < 32, start + lanes, own - 32 + lanes)
+        one_hot = jnp.where(index == wanted, 1.0, 0.0).astype(bf16)
+        block = jnp.dot(halves, one_hot, preferred_element_type=f32)
+        chosen[h, SEC_BLOCKS - 1] = block.astype(bf16)
+        chosen[h, SEC_REACH : SEC_REACH + SEC_OWN] = reach[pl.ds(own // 2, SEC_OWN)]
+
+    def far_copy(first, last, i):
+        return pltpu.make_async_remote_copy(
+            src_ref=chosen.at[1, pl.ds(first, last - first)], dst_ref=far.at[pl.ds(first, last - first)],
+            send_sem=far_send.at[i], recv_sem=far_recv.at[i], device_id=across, device_id_type=MESH,
+        )
+
+    far_early = far_copy(SEC_REACH, SEC_BLOCKS, 0)
+    far_early.start()
+
     for i, d in enumerate((1, 3, 2)):
         x_copies[i].wait_recv()
         copy = c_copy(0, (x - d + 4) % 4, 1 + i)
@@ -190,22 +208,44 @@
         for i in range(4):
             c_copy(1, (x - i + 4) % 4, 4 + i).wait()
 
-    s_copies = []
-    for k, (a, b) in enumerate(members):
-        to_zh, to_y = (zh + a) % 2, (y + b) % 4
-        own = wp * 16 + to_zh * 8 + to_y * 2
-        first = own + off_ref[to_zh] // 2
-        sending[k, :REACH_PAIRS] = reach[pl.ds(first, REACH_PAIRS)]
-        sending[k, REACH_PAIRS : REACH_PAIRS + OWN_PAIRS] = reach[pl.ds(own, OWN_PAIRS)]
-        if k < 7:
-            copy = pltpu.make_async_remote_copy(
-                src_ref=sending.at[k], dst_ref=out_hbm.at[shot], send_sem=s_send.at[k], recv_sem=s_recv.at[k],
-                device_id=(well, shot_peers[k]), device_id_type=MESH,
-            )
-        else:
-            copy = pltpu.make_async_copy(sending.at[k], out_hbm.at[shot], load_sem.at[3])
-        copy.start()
-        s_copies.append(copy)
+    for h in (1, 0):
+        first = wp * 16 + (zh + h) % 2 * 8 + off_ref[(zh + h) % 2] // 2
+        chosen[h, :SEC_REACH] = reach[pl.ds(first, SEC_REACH)]
+        if h == 1:
+            far_late = far_copy(0, SEC_REACH, 1)
+            far_late.start()
+
+    def parts(source, from_shot, to_y):
+        return [
+            (source.at[pl.ds(2 * to_y, REACH_PAIRS)], out_hbm.at[from_shot, pl.ds(0, REACH_PAIRS)]),
+            (source.at[pl.ds(SEC_REACH + 2 * to_y, OWN_PAIRS)], out_hbm.at[from_shot, pl.ds(REACH_PAIRS, OWN_PAIRS)]),
+            (source.at[pl.ds(SEC_BLOCKS - 1, 1)], out_hbm.at[from_shot, pl.ds(BLOCKS - 1, 1)]),
+        ]
+
+    waiting = []
+
+    def pass_on(source, from_shot, h, kinds):
+        for i, peer in enumerate(y_peers):
+            pieces = parts(source, from_shot, peer)
+            for kind in kinds:
+                n = (h * 3 + i) * 3 + kind
+                copy = pltpu.make_async_remote_copy(
+                    src_ref=pieces[kind][0], dst_ref=pieces[kind][1], send_sem=y_send.at[n], recv_sem=y_recv.at[n],
+                    device_id=(well, zh * 4 + peer), device_id_type=MESH,
+                )
+                copy.start()
+                waiting.append(copy)
+        pieces = parts(source, from_shot, y)
+        for kind in kinds:
+            copy = pltpu.make_async_copy(pieces[kind][0], pieces[kind][1], keep_sem.at[h * 3 + kind])
+            copy.start()
+            waiting.append(copy)
+
+    pass_on(chosen.at[0], shot, 0, (0, 1, 2))
+    far_early.wait_recv()
+    pass_on(far, far_shot, 1, (1, 2))
+    far_late.wait_recv()
+    pass_on(far, far_shot, 1, (0,))
     for copy in x_copies:
         copy.wait_send()
 
@@ -214,7 +254,9 @@
         for i in range(4):
             z_copy(i).wait_send()
 
-    for copy in s_copies:
+    far_early.wait_send()
+    far_late.wait_send()
+    for copy in waiting:
         copy.wait()
 
 
@@ -251,14 +293,15 @@
     return parts[0]
 
 
-def cross_kernel(off_ref, data, table, out, flat, gate_vals, spectra):
+def cross_kernel(off_hbm, data, table, out, off_ref, flat, gate_vals, spectra, sem):
     z, wp, zh, y = place()
-    odd = off_ref[zh] & 1
+    load_off = pltpu.make_async_copy(off_hbm, off_ref, sem)
+    load_off.start()
     lane = lax.broadcasted_iota(jnp.int32, (8, W), 1)
     lane_f = lane.astype(f32)
 
     for k in range(8):
-        block = data[k, BLOCKS - 1].astype(f32)
+        block = pltpu.roll(data[k, BLOCKS - 1].astype(f32), (W - 4 * y) % W, 1)
         gate = block[:8] * 8.0 + block[8:]
         step_cos, step_sin = turn(fraction(gate * 0.125))
         for slot in range(SLOTS):
@@ -296,6 +339,9 @@
                             cosine * step_cos - sine * step_sin,
                             sine * step_cos + cosine * step_sin,
                         )
+
+    load_off.wait()
+    odd = off_ref[zh] & 1
 
     @pl.loop(0, 4)
     def _(a):
@@ -340,37 +386,41 @@
 
 def local(traces, gate_starts, section_offsets):
     any_space = pl.BlockSpec(memory_space=pl.ANY)
-    smem = pl.BlockSpec(memory_space=pltpu.SMEM)
     vmem = pl.BlockSpec(memory_space=pltpu.VMEM)
     dma = pltpu.SemaphoreType.DMA
     arrived = pl.pallas_call(
         gather_kernel,
         out_shape=jax.ShapeDtypeStruct((8, BLOCKS, 16, W), bf16),
-        in_specs=[smem, any_space, any_space],
+        in_specs=[any_space, any_space, any_space],
         out_specs=any_space,
         scratch_shapes=[
+            pltpu.SMEM((2,), jnp.int32),
             pltpu.VMEM((8, RECV, NT), bf16),
             pltpu.VMEM((8, 512), jnp.int32),
             pltpu.VMEM((256, 8), f32),
             pltpu.VMEM((RECV * 8, W), f32),
             pltpu.VMEM((256, 16, W), bf16),
-            pltpu.VMEM((8, BLOCKS, 16, W), bf16),
-            dma((4,)), dma((3,)), dma((3,)), dma((4,)), dma((4,)), dma((8,)), dma((8,)), dma((7,)), dma((7,)),
+            pltpu.VMEM((2, SEC_BLOCKS, 16, W), bf16),
+            pltpu.VMEM((SEC_BLOCKS, 16, W), bf16),
+            dma((3,)), dma((8,)), dma((3,)), dma((3,)), dma((4,)), dma((4,)), dma((8,)), dma((8,)),
+            dma((2,)), dma((2,)), dma((18,)), dma((18,)), dma((6,)),
         ],
         compiler_params=pltpu.CompilerParams(
-            collective_id=0, has_side_effects=True, vmem_limit_bytes=16 * 2**20
+            collective_id=0, has_side_effects=True, vmem_limit_bytes=60 * 2**20
         ),
         name="gather",
     )(section_offsets, traces, gate_starts)
     return pl.pallas_call(
         cross_kernel,
         out_shape=jax.ShapeDtypeStruct((4, PARTNERS, NT + 2), f32),
-        in_specs=[smem, vmem, vmem],
+        in_specs=[any_space, vmem, vmem],
         out_specs=vmem,
         scratch_shapes=[
+            pltpu.SMEM((2,), jnp.int32),
             pltpu.VMEM((128, NT), f32),
             pltpu.VMEM((SLOTS, 8, 3, 8, W), f32),
             pltpu.VMEM((SLOTS, 4, 2, 64, W), f32),
+            dma,
         ],
         compiler_params=pltpu.CompilerParams(vmem_limit_bytes=32 * 2**20),
         name="cross",

time: 60 us -> 53.3 us (0.89)
  the two profiles are of different devices: /device:TPU:32 before, /device:TPU:1 now
where the time goes in v2:
time: 53.3 us; the launch traced here: 53.1 us
  Pallas kernels  52.1 us (98%)
  local copies, waits for them, and re-layouts  1.01 us (2%)
    pallas_call x1, Pallas kernels, local(): pl.pallas_call(gather_kernel, out_shape=jax.ShapeDtypeStruct((8, BLOCKS,...  43.8 us
    pallas_call x1, Pallas kernels, local(): pl.pallas_call(cross_kernel, out_shape=jax.ShapeDtypeStruct((4, PARTNERS,...  8.3 us

profile of v2, /device:TPU:1, one launch (start us, length us, event | category | flops | bytes accessed | tf_op | source)
XLA Modules:
  0.0 53.1 jit_solution(1361509499100888090)
XLA Ops:
  0.0 0.0 copy-start.1
  0.0 0.0 copy-start.2
  0.0 43.8 %gather.1.data = bf16[8,13,16,128]{3,2,1,0:T(8,128)(2,1)} custom-call(s32[2]{0:T(128)} %off_hbm.3, bf16[8,32,1024]{2,1,0:T(8,128)(2,1)} %traces_hbm.1, s32[8,2048]{1,0:T(8,128)} %gates_hbm.1), custom_call_target="tpu_custom_call" | custom-call | tf_op jit(solution)/shard_map/gather/pallas_call | solution.py:391
  43.8 0.0 copy-done.1
  43.8 0.0 copy-done.2
  43.8 0.0 copy-start
  43.8 1.0 %copy-done = bf16[8,13,16,128]{3,2,1,0:T(8,128)(2,1)S(1)} copy-done((bf16[8,13,16,128]{3,2,1,0:T(8,128)(2,1)S(1)}, bf16[8,13,16,128]{3,2,1,0:T(8,128)(2,1)}, u32[]{:S(2)}) %copy-start) | copy-done | bytes 426008
  44.8 8.3 %cross.1 = f32[4,16,1026]{2,1,0:T(8,128)} custom-call(s32[2]{0:T(128)S(1)} %copy-done.2, bf16[8,13,16,128]{3,2,1,0:T(8,128)(2,1)S(1)} %copy-done, bf16[128,1024]{1,0:T(8,128)(2,1)S(1)} %copy-done.1), custom_call_target="tpu_custom_call" | custom-call | tf_op jit(solution)/shard_map/cross/pallas_call | solution.py:413
Async XLA Ops:
  0.0 43.8 %copy-start.1 = (bf16[128,1024]{1,0:T(8,128)(2,1)S(1)}, bf16[128,1024]{1,0:T(8,128)(2,1)}, u32[]{:S(2)}) copy-start(bf16[128,1024]{1,0:T(8,128)(2,1)} %constant.2.clone.table) | copy-start | bytes 786436
  0.0 43.8 %copy-start.2 = (s32[2]{0:T(128)S(1)}, s32[2]{0:T(128)}, u32[]{:S(2)}) copy-start(s32[2]{0:T(128)} %off_hbm.3) | copy-start | bytes 28
  43.8 1.0 %copy-start = (bf16[8,13,16,128]{3,2,1,0:T(8,128)(2,1)S(1)}, bf16[8,13,16,128]{3,2,1,0:T(8,128)(2,1)}, u32[]{:S(2)}) copy-start(bf16[8,13,16,128]{3,2,1,0:T(8,128)(2,1)} %gather.1.data) | copy-start | bytes 1277956

commit v3 on v2

--- a/solution.py
+++ b/solution.py
@@ -21,7 +21,7 @@
 BLOCKS = REACH_PAIRS + OWN_PAIRS + 1
 SEC_REACH = 16
 SEC_OWN = 8
-SEC_BLOCKS = SEC_REACH + SEC_OWN + 1
+CLASSES = 8
 SLOTS = 2 * (REACH_PAIRS + OWN_PAIRS)
 MESH = pl.DeviceIdType.MESH
 f32 = jnp.float32
@@ -46,53 +46,53 @@
 
 def gather_kernel(
     off_hbm, traces_hbm, gates_hbm, out_hbm,
-    off_ref, traces, gates, gate_cols, rows, reach, chosen, far,
-    load_sem, trace_sem, x_send, x_recv, z_send, z_recv, c_send, c_recv,
-    far_send, far_recv, y_send, y_recv, keep_sem,
+    offs, traces, gates, gate_cols, rows, unit, dealt, held, picked, landed, far_landed, ordered, extra, far_extra,
+    load_sem, o_send, o_recv, a_send, a_recv, z_send, z_recv, n_send, n_recv,
+    f_send, f_recv, e_send, e_recv, y_send, y_recv, keep_sem,
 ):
     z, wp, zh, y = place()
     x, core = wp // 2, wp % 2
     well = z * PLANE + wp
     shot = zh * 4 + y
     far_shot = (1 - zh) * 4 + y
-
-    def well_at(plane, column, which):
-        return plane * PLANE + column * 2 + which
-
-    x_peers = [(x + d) % 4 for d in (1, 3, 2)]
+    before = jnp.maximum(z - 1, 0)
+
+    steps = [(dx, dc) for dx in (0, 1, 3, 2) for dc in (0, 1)]
+    near = [(x + dx) % 4 * 2 + (core + dc) % 2 for dx, dc in steps]
     y_peers = [(y + d) % 4 for d in (1, 3, 2)]
-    other_core = (well_at(z, x, 1 - core), shot)
-    across = (well, far_shot)
 
     barrier = pltpu.get_barrier_semaphore()
-    pl.semaphore_signal(barrier, inc=1, device_id=across, device_id_type=MESH)
-    for column in x_peers:
-        pl.semaphore_signal(barrier, inc=1, device_id=(well_at(z, column, core), shot), device_id_type=MESH)
+
+    def greet(to_well, to_shot):
+        pl.semaphore_signal(barrier, inc=1, device_id=(to_well, to_shot), device_id_type=MESH)
+
+    for peer in near:
+        greet(z * PLANE + peer, far_shot)
 
     @pl.when(z < 7)
     def _():
-        for column in range(4):
-            pl.semaphore_signal(barrier, inc=1, device_id=(well_at(z + 1, column, core), shot), device_id_type=MESH)
-
+        for peer in near:
+            greet((z + 1) * PLANE + peer, shot)
+
+    for peer in near[1:]:
+        greet(z * PLANE + peer, shot)
     for peer in y_peers:
-        pl.semaphore_signal(barrier, inc=1, device_id=(well, zh * 4 + peer), device_id_type=MESH)
-    pl.semaphore_signal(barrier, inc=1, device_id=other_core, device_id_type=MESH)
+        greet(well, zh * 4 + peer)
 
     here = pl.multiple_of(z * 256, 256)
     ahead = pl.multiple_of(jnp.minimum(z + 1, 7) * 256, 256)
     load_here = pltpu.make_async_copy(gates_hbm.at[:, pl.ds(here, 256)], gates.at[:, pl.ds(0, 256)], load_sem.at[0])
     load_ahead = pltpu.make_async_copy(gates_hbm.at[:, pl.ds(ahead, 256)], gates.at[:, pl.ds(256, 256)], load_sem.at[1])
-    load_off = pltpu.make_async_copy(off_hbm, off_ref, load_sem.at[2])
+    load_off = pltpu.make_async_copy(off_hbm, offs.at[wp], load_sem.at[2])
     load_here.start()
-    load_traces = [pltpu.make_async_copy(traces_hbm.at[s], traces.at[s], trace_sem.at[s]) for s in range(8)]
-    for copy in load_traces:
-        copy.start()
+    load_traces = pltpu.make_async_copy(traces_hbm, traces, load_sem.at[3])
+    load_traces.start()
+    load_off.start()
     load_ahead.start()
-    load_off.start()
 
     @pl.when(z == 7)
     def _():
-        reach[pl.ds(128, 128)] = jnp.zeros((128, 16, W), bf16)
+        held[pl.ds(16, 16)] = jnp.zeros((16, 16, W), bf16)
 
     lane = lax.broadcasted_iota(jnp.int32, (RECV, W), 1)
     taper = 0.5 - 0.5 * jnp.cos((lane[:8].astype(f32) + 0.5) * (2 * math.pi / W))
@@ -100,8 +100,8 @@
     load_here.wait()
     gate_cols[...] = jnp.transpose(gates[:, :256].astype(f32))
     columns = gate_cols[pl.ds(pl.multiple_of(wp * RECV, RECV), RECV), :].astype(jnp.int32)
+    load_traces.wait()
     for s in range(8):
-        load_traces[s].wait()
         data = traces[s].astype(f32)
         gate = jnp.broadcast_to(columns[:, s : s + 1], (RECV, W))
         fine = gate & 127
@@ -118,144 +118,150 @@
             step = 1 << bit
             turned = jnp.where((fine & step) != 0, pltpu.roll(turned, W - step, 1), turned)
         rows[pl.ds(s, RECV, stride=8), :] = turned * taper
-    own_first = pl.multiple_of(wp * 16, 16)
-    reach[pl.ds(own_first, 16)] = rows[...].reshape(16, 16, W).astype(bf16)
+    pairs = rows[...].reshape(16, 16, W).astype(bf16)
+    unit[...] = pairs
+    for i in range(2):
+        for m in range(CLASSES):
+            dealt[m, i] = pairs[i * CLASSES + m]
 
     @pl.when(z > 0)
     def _():
-        pl.semaphore_wait(barrier, 12)
+        pl.semaphore_wait(barrier, 26)
 
     @pl.when(z == 0)
     def _():
-        pl.semaphore_wait(barrier, 8)
-
-    def slot(plane, column, which):
-        first = pl.multiple_of((plane * PLANE + column * 2 + which) * 16, 16)
-        return reach.at[pl.ds(first, 16)]
-
-    mine = slot(0, x, core)
-    x_copies = []
-    for i, column in enumerate(x_peers):
-        copy = pltpu.make_async_remote_copy(
-            src_ref=mine, dst_ref=mine, send_sem=x_send.at[i], recv_sem=x_recv.at[i],
-            device_id=(well_at(z, column, core), shot), device_id_type=MESH,
+        pl.semaphore_wait(barrier, 18)
+
+    def remote(source, target, send, receive, to_well, to_shot):
+        return pltpu.make_async_remote_copy(
+            src_ref=source, dst_ref=target, send_sem=send, recv_sem=receive,
+            device_id=(to_well, to_shot), device_id_type=MESH,
         )
+
+    mine = pl.ds(wp * 2, 2)
+    mine_ahead = pl.ds(16 + wp * 2, 2)
+
+    def z_copy(k):
+        return remote(
+            dealt.at[near[k]], held.at[mine_ahead], z_send.at[k], z_recv.at[k], before * PLANE + near[k], shot
+        )
+
+    @pl.when(z > 0)
+    def _():
+        for k in range(8):
+            z_copy(k).start()
+
+    a_copies = []
+    o_copies = []
+    for k in range(1, 8):
+        to_well = z * PLANE + near[k]
+        copy = remote(dealt.at[near[k]], held.at[mine], a_send.at[k], a_recv.at[k], to_well, shot)
         copy.start()
-        x_copies.append(copy)
-
-    def z_copy(i):
-        return pltpu.make_async_remote_copy(
-            src_ref=mine, dst_ref=slot(1, x, core), send_sem=z_send.at[i], recv_sem=z_recv.at[i],
-            device_id=(well_at(jnp.maximum(z - 1, 0), (x + i) % 4, core), shot), device_id_type=MESH,
-        )
-
-    @pl.when(z > 0)
-    def _():
-        for i in range(4):
-            z_copy(i).start()
-
-    def c_copy(plane, column, i):
-        block = slot(plane, column, core)
-        return pltpu.make_async_remote_copy(
-            src_ref=block, dst_ref=block, send_sem=c_send.at[i], recv_sem=c_recv.at[i],
-            device_id=other_core, device_id_type=MESH,
-        )
-
-    c_copies = [c_copy(0, x, 0)]
-    c_copies[0].start()
+        a_copies.append(copy)
+    load_off.wait()
+    for k in range(1, 8):
+        copy = remote(offs.at[wp], offs.at[wp], o_send.at[k], o_recv.at[k], z * PLANE + near[k], shot)
+        copy.start()
+        o_copies.append(copy)
+    held[mine] = dealt[wp]
 
     load_ahead.wait()
-    load_off.wait()
     all_gates = gates[...]
     halves = jnp.concatenate([all_gates >> 3, all_gates & 7], axis=0).astype(f32).astype(bf16)
     lanes = lax.broadcasted_iota(jnp.int32, (512, W), 1)
     index = lax.broadcasted_iota(jnp.int32, (512, W), 0)
     for h in (1, 0):
-        own = wp * RECV + (zh + h) % 2 * SEC
-        start = (own + off_ref[(zh + h) % 2]) // 2 * 2
+        section = (zh + h) % 2
+        own = wp * RECV + section * SEC
+        start = (own + offs[wp, section]) // 2 * 2
         wanted = jnp.where(lanes < 32, start + lanes, own - 32 + lanes)
         one_hot = jnp.where(index == wanted, 1.0, 0.0).astype(bf16)
         block = jnp.dot(halves, one_hot, preferred_element_type=f32)
-        chosen[h, SEC_BLOCKS - 1] = block.astype(bf16)
-        chosen[h, SEC_REACH : SEC_REACH + SEC_OWN] = reach[pl.ds(own // 2, SEC_OWN)]
-
-    def far_copy(first, last, i):
-        return pltpu.make_async_remote_copy(
-            src_ref=chosen.at[1, pl.ds(first, last - first)], dst_ref=far.at[pl.ds(first, last - first)],
-            send_sem=far_send.at[i], recv_sem=far_recv.at[i], device_id=across, device_id_type=MESH,
-        )
-
-    far_early = far_copy(SEC_REACH, SEC_BLOCKS, 0)
-    far_early.start()
-
-    for i, d in enumerate((1, 3, 2)):
-        x_copies[i].wait_recv()
-        copy = c_copy(0, (x - d + 4) % 4, 1 + i)
+        extra[h, :SEC_OWN] = unit[pl.ds(section * SEC_OWN, SEC_OWN)]
+        extra[h, SEC_OWN] = block.astype(bf16)
+
+    e_copy = remote(extra.at[1], far_extra, e_send, e_recv, well, far_shot)
+    e_copy.start()
+    for copy in o_copies:
+        copy.wait_recv()
+    for copy in a_copies:
+        copy.wait_recv()
+
+    @pl.when(z < 7)
+    def _():
+        for k in range(8):
+            z_copy(k).wait_recv()
+
+    for h in (1, 0):
+        section = (zh + h) % 2
+        for k in range(8):
+            first = near[k] * 16 + section * SEC_OWN + offs[near[k], section] // 2
+            at = (first + (wp + 512 - first) % CLASSES) // CLASSES
+            picked[h, k] = held[pl.ds(at, 2)]
+    f_copies = []
+    n_copies = []
+    for k in range(8):
+        to_well = z * PLANE + near[k]
+        copy = remote(picked.at[1, k], far_landed.at[wp], f_send.at[k], f_recv.at[k], to_well, far_shot)
         copy.start()
-        c_copies.append(copy)
-
-    @pl.when(z < 7)
-    def _():
-        for i in range(4):
-            z_copy(i).wait_recv()
-            c_copy(1, (x - i + 4) % 4, 4 + i).start()
-
-    for i in range(4):
-        c_copies[i].wait()
-
-    @pl.when(z < 7)
-    def _():
-        for i in range(4):
-            c_copy(1, (x - i + 4) % 4, 4 + i).wait()
-
-    for h in (1, 0):
-        first = wp * 16 + (zh + h) % 2 * 8 + off_ref[(zh + h) % 2] // 2
-        chosen[h, :SEC_REACH] = reach[pl.ds(first, SEC_REACH)]
-        if h == 1:
-            far_late = far_copy(0, SEC_REACH, 1)
-            far_late.start()
-
-    def parts(source, from_shot, to_y):
-        return [
-            (source.at[pl.ds(2 * to_y, REACH_PAIRS)], out_hbm.at[from_shot, pl.ds(0, REACH_PAIRS)]),
-            (source.at[pl.ds(SEC_REACH + 2 * to_y, OWN_PAIRS)], out_hbm.at[from_shot, pl.ds(REACH_PAIRS, OWN_PAIRS)]),
-            (source.at[pl.ds(SEC_BLOCKS - 1, 1)], out_hbm.at[from_shot, pl.ds(BLOCKS - 1, 1)]),
-        ]
-
+        f_copies.append(copy)
+    for k in range(1, 8):
+        to_well = z * PLANE + near[k]
+        copy = remote(picked.at[0, k], landed.at[wp], n_send.at[k], n_recv.at[k], to_well, shot)
+        copy.start()
+        n_copies.append(copy)
+    landed[wp] = picked[0, 0]
+
+    own_first = wp * 16 + zh * SEC_OWN + offs[wp, zh] // 2
     waiting = []
 
-    def pass_on(source, from_shot, h, kinds):
+    def pass_on(h, kinds):
+        from_shot = (far_shot if h else shot)
+        more = far_extra if h else extra.at[0]
+
+        def pieces(to_y):
+            return [
+                (ordered.at[h, pl.ds(2 * to_y, REACH_PAIRS)], out_hbm.at[from_shot, pl.ds(0, REACH_PAIRS)]),
+                (more.at[pl.ds(2 * to_y, OWN_PAIRS)], out_hbm.at[from_shot, pl.ds(REACH_PAIRS, OWN_PAIRS)]),
+                (more.at[pl.ds(SEC_OWN, 1)], out_hbm.at[from_shot, pl.ds(BLOCKS - 1, 1)]),
+            ]
+
         for i, peer in enumerate(y_peers):
-            pieces = parts(source, from_shot, peer)
             for kind in kinds:
                 n = (h * 3 + i) * 3 + kind
-                copy = pltpu.make_async_remote_copy(
-                    src_ref=pieces[kind][0], dst_ref=pieces[kind][1], send_sem=y_send.at[n], recv_sem=y_recv.at[n],
-                    device_id=(well, zh * 4 + peer), device_id_type=MESH,
-                )
+                source, target = pieces(peer)[kind]
+                copy = remote(source, target, y_send.at[n], y_recv.at[n], well, zh * 4 + peer)
                 copy.start()
                 waiting.append(copy)
-        pieces = parts(source, from_shot, y)
         for kind in kinds:
-            copy = pltpu.make_async_copy(pieces[kind][0], pieces[kind][1], keep_sem.at[h * 3 + kind])
+            source, target = pieces(y)[kind]
+            copy = pltpu.make_async_copy(source, target, keep_sem.at[h * 3 + kind])
             copy.start()
             waiting.append(copy)
 
-    pass_on(chosen.at[0], shot, 0, (0, 1, 2))
-    far_early.wait_recv()
-    pass_on(far, far_shot, 1, (1, 2))
-    far_late.wait_recv()
-    pass_on(far, far_shot, 1, (0,))
-    for copy in x_copies:
+    def put_in_order(h, arrived):
+        for i in range(SEC_REACH):
+            ordered[h, i] = arrived[(own_first + i) % CLASSES, i // CLASSES]
+
+    pass_on(0, (1, 2))
+    for copy in n_copies:
+        copy.wait_recv()
+    put_in_order(0, landed)
+    pass_on(0, (0,))
+    e_copy.wait_recv()
+    pass_on(1, (1, 2))
+    for copy in f_copies:
+        copy.wait_recv()
+    put_in_order(1, far_landed)
+    pass_on(1, (0,))
+
+    @pl.when(z > 0)
+    def _():
+        for k in range(8):
+            z_copy(k).wait_send()
+
+    for copy in a_copies + o_copies + n_copies + f_copies + [e_copy]:
         copy.wait_send()
-
-    @pl.when(z > 0)
-    def _():
-        for i in range(4):
-            z_copy(i).wait_send()
-
-    far_early.wait_send()
-    far_late.wait_send()
     for copy in waiting:
         copy.wait()
 
@@ -394,16 +400,22 @@
         in_specs=[any_space, any_space, any_space],
         out_specs=any_space,
         scratch_shapes=[
-            pltpu.SMEM((2,), jnp.int32),
+            pltpu.SMEM((PLANE, 2), jnp.int32),
             pltpu.VMEM((8, RECV, NT), bf16),
             pltpu.VMEM((8, 512), jnp.int32),
             pltpu.VMEM((256, 8), f32),
             pltpu.VMEM((RECV * 8, W), f32),
-            pltpu.VMEM((256, 16, W), bf16),
-            pltpu.VMEM((2, SEC_BLOCKS, 16, W), bf16),
-            pltpu.VMEM((SEC_BLOCKS, 16, W), bf16),
-            dma((3,)), dma((8,)), dma((3,)), dma((3,)), dma((4,)), dma((4,)), dma((8,)), dma((8,)),
-            dma((2,)), dma((2,)), dma((18,)), dma((18,)), dma((6,)),
+            pltpu.VMEM((16, 16, W), bf16),
+            pltpu.VMEM((CLASSES, 2, 16, W), bf16),
+            pltpu.VMEM((32, 16, W), bf16),
+            pltpu.VMEM((2, PLANE, 2, 16, W), bf16),
+            pltpu.VMEM((CLASSES, 2, 16, W), bf16),
+            pltpu.VMEM((CLASSES, 2, 16, W), bf16),
+            pltpu.VMEM((2, SEC_REACH, 16, W), bf16),
+            pltpu.VMEM((2, SEC_OWN + 1, 16, W), bf16),
+            pltpu.VMEM((SEC_OWN + 1, 16, W), bf16),
+            dma((4,)), dma((8,)), dma((8,)), dma((8,)), dma((8,)), dma((8,)), dma((8,)),
+            dma((8,)), dma((8,)), dma((8,)), dma((8,)), dma, dma, dma((18,)), dma((18,)), dma((6,)),
         ],
         compiler_params=pltpu.CompilerParams(
             collective_id=0, has_side_effects=True, vmem_limit_bytes=60 * 2**20

time: 53.3 us -> 45.6 us (0.86)
  the two profiles are of different devices: /device:TPU:1 before, /device:TPU:36 now
where the time goes in v3:
time: 45.6 us; the launch traced here: 45.4 us
  Pallas kernels  44.4 us (97%)
  local copies, waits for them, and re-layouts  1.01 us (2%)
    pallas_call x1, Pallas kernels, local(): pl.pallas_call(gather_kernel, out_shape=jax.ShapeDtypeStruct((8, BLOCKS,...  36.1 us
    pallas_call x1, Pallas kernels, local(): pl.pallas_call(cross_kernel, out_shape=jax.ShapeDtypeStruct((4, PARTNERS,...  8.3 us
    unnamed x6, local copies, waits for them, and re-layouts  1.01 us

profile of v3, /device:TPU:36, one launch (start us, length us, event | category | flops | bytes accessed | tf_op | source)
XLA Modules:
  0.0 45.4 jit_solution(9797922378131571815)
XLA Ops:
  0.0 0.0 copy-start.1
  0.0 0.0 copy-start.2
  0.0 36.1 %gather.1.data = bf16[8,13,16,128]{3,2,1,0:T(8,128)(2,1)} custom-call(s32[2]{0:T(128)} %off_hbm.3, bf16[8,32,1024]{2,1,0:T(8,128)(2,1)} %traces_hbm.1, s32[8,2048]{1,0:T(8,128)} %gates_hbm.1), custom_call_target="tpu_custom_call" | custom-call | tf_op jit(solution)/shard_map/gather/pallas_call | solution.py:397
  36.1 0.0 copy-done.1
  36.1 0.0 copy-done.2
  36.1 0.0 copy-start
  36.1 1.0 %copy-done = bf16[8,13,16,128]{3,2,1,0:T(8,128)(2,1)S(1)} copy-done((bf16[8,13,16,128]{3,2,1,0:T(8,128)(2,1)S(1)}, bf16[8,13,16,128]{3,2,1,0:T(8,128)(2,1)}, u32[]{:S(2)}) %copy-start) | copy-done | bytes 426008
  37.1 8.3 %cross.1 = f32[4,16,1026]{2,1,0:T(8,128)} custom-call(s32[2]{0:T(128)S(1)} %copy-done.2, bf16[8,13,16,128]{3,2,1,0:T(8,128)(2,1)S(1)} %copy-done, bf16[128,1024]{1,0:T(8,128)(2,1)S(1)} %copy-done.1), custom_call_target="tpu_custom_call" | custom-call | tf_op jit(solution)/shard_map/cross/pallas_call | solution.py:425
Async XLA Ops:
  0.0 36.1 %copy-start.1 = (bf16[128,1024]{1,0:T(8,128)(2,1)S(1)}, bf16[128,1024]{1,0:T(8,128)(2,1)}, u32[]{:S(2)}) copy-start(bf16[128,1024]{1,0:T(8,128)(2,1)} %constant.2.clone.table) | copy-start | bytes 786436
  0.0 36.1 %copy-start.2 = (s32[2]{0:T(128)S(1)}, s32[2]{0:T(128)}, u32[]{:S(2)}) copy-start(s32[2]{0:T(128)} %off_hbm.3) | copy-start | bytes 28
  36.1 1.0 %copy-start = (bf16[8,13,16,128]{3,2,1,0:T(8,128)(2,1)S(1)}, bf16[8,13,16,128]{3,2,1,0:T(8,128)(2,1)}, u32[]{:S(2)}) copy-start(bf16[8,13,16,128]{3,2,1,0:T(8,128)(2,1)} %gather.1.data) | copy-start | bytes 1277956

commit v4 on v3

--- a/solution.py
+++ b/solution.py
@@ -28,7 +28,7 @@
 bf16 = jnp.bfloat16
 
 def packed_table():
-    steps = np.arange(W)
+    steps = np.arange(2 * W)
     k = np.arange(NT // 2)
     angle = ((steps[:, None] * k[None, :]) % NT).astype(np.float32) * np.float32(2 * math.pi / NT)
     real = np.cos(angle)
@@ -45,7 +45,8 @@
 
 
 def gather_kernel(
-    off_hbm, traces_hbm, gates_hbm, out_hbm,
+    off_hbm, traces_hbm, gates_hbm, table_hbm, far_hbm, part_hbm,
+    near_in, table, gate_vals, spectra, part,
     offs, traces, gates, gate_cols, rows, unit, dealt, held, picked, landed, far_landed, ordered, extra, far_extra,
     load_sem, o_send, o_recv, a_send, a_recv, z_send, z_recv, n_send, n_recv,
     f_send, f_recv, e_send, e_recv, y_send, y_recv, keep_sem,
@@ -89,6 +90,8 @@
     load_traces.start()
     load_off.start()
     load_ahead.start()
+    load_table = pltpu.make_async_copy(table_hbm, table, load_sem.at[4])
+    load_table.start()
 
     @pl.when(z == 7)
     def _():
@@ -114,10 +117,10 @@
         low = jnp.where(pick, three[1], three[0])
         high = jnp.where(pick, three[2], three[1])
         turned = jnp.where(lane >= fine, low, high)
-        for bit in range(7):
+        for bit in range(3, 7):
             step = 1 << bit
             turned = jnp.where((fine & step) != 0, pltpu.roll(turned, W - step, 1), turned)
-        rows[pl.ds(s, RECV, stride=8), :] = turned * taper
+        rows[pl.ds(s, RECV, stride=8), :] = turned * jnp.take_along_axis(taper, (lane - (gate & 7)) & 127, axis=1)
     pairs = rows[...].reshape(16, 16, W).astype(bf16)
     unit[...] = pairs
     for i in range(2):
@@ -213,47 +216,63 @@
     landed[wp] = picked[0, 0]
 
     own_first = wp * 16 + zh * SEC_OWN + offs[wp, zh] // 2
-    waiting = []
 
     def pass_on(h, kinds):
-        from_shot = (far_shot if h else shot)
+        target = (far_hbm if h else near_in).at[y]
         more = far_extra if h else extra.at[0]
 
         def pieces(to_y):
             return [
-                (ordered.at[h, pl.ds(2 * to_y, REACH_PAIRS)], out_hbm.at[from_shot, pl.ds(0, REACH_PAIRS)]),
-                (more.at[pl.ds(2 * to_y, OWN_PAIRS)], out_hbm.at[from_shot, pl.ds(REACH_PAIRS, OWN_PAIRS)]),
-                (more.at[pl.ds(SEC_OWN, 1)], out_hbm.at[from_shot, pl.ds(BLOCKS - 1, 1)]),
+                (ordered.at[h, pl.ds(2 * to_y, REACH_PAIRS)], target.at[pl.ds(0, REACH_PAIRS)]),
+                (more.at[pl.ds(2 * to_y, OWN_PAIRS)], target.at[pl.ds(REACH_PAIRS, OWN_PAIRS)]),
+                (more.at[pl.ds(SEC_OWN, 1)], target.at[pl.ds(BLOCKS - 1, 1)]),
             ]
 
+        copies = []
         for i, peer in enumerate(y_peers):
             for kind in kinds:
                 n = (h * 3 + i) * 3 + kind
-                source, target = pieces(peer)[kind]
-                copy = remote(source, target, y_send.at[n], y_recv.at[n], well, zh * 4 + peer)
-                copy.start()
-                waiting.append(copy)
+                source, to = pieces(peer)[kind]
+                copies.append(remote(source, to, y_send.at[n], y_recv.at[n], well, zh * 4 + peer))
         for kind in kinds:
-            source, target = pieces(y)[kind]
-            copy = pltpu.make_async_copy(source, target, keep_sem.at[h * 3 + kind])
+            source, to = pieces(y)[kind]
+            copies.append(pltpu.make_async_copy(source, to, keep_sem.at[h * 3 + kind]))
+        for copy in copies:
             copy.start()
-            waiting.append(copy)
+        return copies
 
     def put_in_order(h, arrived):
         for i in range(SEC_REACH):
             ordered[h, i] = arrived[(own_first + i) % CLASSES, i // CLASSES]
 
-    pass_on(0, (1, 2))
+    near_copies = pass_on(0, (1, 2))
     for copy in n_copies:
         copy.wait_recv()
     put_in_order(0, landed)
-    pass_on(0, (0,))
+    near_copies += pass_on(0, (0,))
     e_copy.wait_recv()
-    pass_on(1, (1, 2))
+    far_copies = pass_on(1, (1, 2))
     for copy in f_copies:
         copy.wait_recv()
     put_in_order(1, far_landed)
-    pass_on(1, (0,))
+    far_copies += pass_on(1, (0,))
+
+    for copy in near_copies:
+        copy.wait()
+    load_table.wait()
+    make_spectra(near_in, table, gate_vals, spectra, y)
+
+    def keep(a, group, reals, imags):
+        rows = pl.ds(group * 8, 8)
+        for t in range(4):
+            part[a, t, rows] = reals[t]
+        for t in range(5):
+            part[a, 4 + t, rows] = imags[t]
+
+    pair_sums(spectra, offs[wp, zh] % 2, keep)
+    keep_part = pltpu.make_async_copy(part, part_hbm, load_sem.at[5])
+    keep_part.start()
+    keep_part.wait()
 
     @pl.when(z > 0)
     def _():
@@ -262,22 +281,8 @@
 
     for copy in a_copies + o_copies + n_copies + f_copies + [e_copy]:
         copy.wait_send()
-    for copy in waiting:
+    for copy in far_copies:
         copy.wait()
-
-
-def turn(angle):
-    half = angle * math.pi
-    sq = half * half
-    sine = half * (1.0 + sq * (-1 / 6 + sq * (1 / 120 + sq * (-1 / 5040 + sq * (1 / 362880 - sq * (1 / 39916800))))))
-    cosine = 1.0 + sq * (
-        -0.5 + sq * (1 / 24 + sq * (-1 / 720 + sq * (1 / 40320 + sq * (-1 / 3628800 + sq * (1 / 479001600)))))
-    )
-    return 1.0 - 2.0 * sine * sine, 2.0 * sine * cosine
-
-
-def fraction(value):
-    return value - jnp.round(value)
 
 
 def fold(parts):
@@ -299,67 +304,63 @@
     return parts[0]
 
 
-def cross_kernel(off_hbm, data, table, out, off_ref, flat, gate_vals, spectra, sem):
-    z, wp, zh, y = place()
-    load_off = pltpu.make_async_copy(off_hbm, off_ref, sem)
-    load_off.start()
+def make_spectra(data, table, gate_vals, spectra, y):
     lane = lax.broadcasted_iota(jnp.int32, (8, W), 1)
-    lane_f = lane.astype(f32)
-
-    for k in range(8):
+    angle = lane.astype(f32) * (2 * math.pi / W)
+    cosines = jnp.cos(angle)
+    sines = jnp.sin(angle)
+
+    for k in range(4):
         block = pltpu.roll(data[k, BLOCKS - 1].astype(f32), (W - 4 * y) % W, 1)
-        gate = block[:8] * 8.0 + block[8:]
-        step_cos, step_sin = turn(fraction(gate * 0.125))
+        gate = (block[:8] * 8.0 + block[8:]).astype(jnp.int32)
         for slot in range(SLOTS):
             column = slot if slot < 20 else 12 + slot
-            for i, value in enumerate((gate, step_cos, step_sin)):
-                gate_vals[slot, k, i] = jnp.broadcast_to(value[:, column : column + 1], (8, W))
-
-    @pl.loop(0, SLOTS // 2)
-    def _(p):
-        left = data[:, p].reshape(8 * 16, W)
-        flat[...] = jnp.dot(left, table[...], preferred_element_type=f32)
-        for par in range(2):
-            slot = 2 * p + par
-            for k in range(8):
-                first = k * 16 + par * 8
-                gate = gate_vals[slot, k, 0]
-                step_cos = gate_vals[slot, k, 1]
-                step_sin = gate_vals[slot, k, 2]
-                cosine, sine = turn(fraction(gate * (lane_f * (1.0 / NT))))
-                for t in range(4):
-                    real = flat[first : first + 8, t * W : (t + 1) * W]
-                    imag = flat[first : first + 8, (4 + t) * W : (5 + t) * W]
-                    if t == 0:
-                        alternating = 1.0 - 2.0 * jnp.abs(gate - 2.0 * jnp.floor(gate * 0.5))
-                        imag_cos = jnp.where(lane == 0, alternating, cosine)
-                    else:
-                        imag_cos = cosine
-                    new_real = cosine * real + sine * imag
-                    new_imag = imag_cos * imag - sine * real
+            gate_vals[slot, k] = jnp.broadcast_to(gate[:, column : column + 1], (8, W))
+
+    @pl.loop(0, SLOTS // 4)
+    def _(step):
+        lefts = []
+        for p in range(2):
+            for k in range(4):
+                both = data[k, 2 * step + p].astype(f32)
+                halves = []
+                for par in range(2):
+                    window = both[par * 8 : par * 8 + 8]
+                    low = jnp.where(lane >= (gate_vals[4 * step + 2 * p + par, k] & 7), window, 0.0)
+                    halves.append(jnp.concatenate([low, window - low], axis=1))
+                lefts.append(jnp.concatenate(halves, axis=0).astype(bf16))
+        flat = jnp.dot(jnp.concatenate(lefts, axis=0), table[...], preferred_element_type=f32)
+        for p in range(2):
+            for par in range(2):
+                slot = 4 * step + 2 * p + par
+                for k in range(4):
+                    first = p * 64 + k * 16 + par * 8
+                    index = ((gate_vals[slot, k] >> 3) * lane) & 127
+                    cosine = jnp.take_along_axis(cosines, index, axis=1)
+                    sine = jnp.take_along_axis(sines, index, axis=1)
                     rows = slice(k * 8, k * 8 + 8)
-                    spectra[slot, t, 0, rows, :] = new_real.astype(bf16).astype(f32)
-                    spectra[slot, t, 1, rows, :] = new_imag.astype(bf16).astype(f32)
-                    if t < 3:
-                        cosine, sine = (
-                            cosine * step_cos - sine * step_sin,
-                            sine * step_cos + cosine * step_sin,
-                        )
-
-    load_off.wait()
-    odd = off_ref[zh] & 1
+                    for t in range(4):
+                        real = flat[first : first + 8, t * W : (t + 1) * W]
+                        imag = flat[first : first + 8, (4 + t) * W : (5 + t) * W]
+                        spectra[slot, t, 0, rows, :] = cosine * real + sine * imag
+                        spectra[slot, t, 1, rows, :] = cosine * imag - sine * real
+
+
+def pair_sums(spectra, odd, emit):
+    lane = lax.broadcasted_iota(jnp.int32, (8, W), 1)
 
     @pl.loop(0, 4)
     def _(a):
-        imags = []
+        reals = [[], []]
+        imags = [[], []]
         for t in range(4):
-            own = [(spectra[20 + a, t, 0, k * 8 : k * 8 + 8, :], spectra[20 + a, t, 1, k * 8 : k * 8 + 8, :]) for k in range(8)]
+            own = [[spectra[20 + a, t, c, k * 8 : k * 8 + 8, :] for c in range(2)] for k in range(4)]
             for group in range(2):
                 sums = []
                 for j in range(8):
                     slot = a + odd + group * 8 + j
                     one = two = three = None
-                    for k in range(8):
+                    for k in range(4):
                         re = spectra[slot, t, 0, k * 8 : k * 8 + 8, :]
                         im = spectra[slot, t, 1, k * 8 : k * 8 + 8, :]
                         first = own[k][0] * re
@@ -369,37 +370,65 @@
                         two = second if two is None else two + second
                         three = third if three is None else three + third
                     sums.append((one, two, three))
-                rows = pl.ds(group * 8, 8)
+                threes = fold([s[2] for s in sums])
                 if t == 0:
                     ones = fold([s[0] for s in sums])
                     twos = fold([s[1] for s in sums])
-                    threes = fold([s[2] for s in sums])
-                    out[a, rows, :W] = jnp.where(lane == 0, ones, ones + twos)
-                    imags.append((twos, jnp.where(lane == 0, 0.0, threes)))
+                    reals[group].append(jnp.where(lane == 0, ones, ones + twos))
+                    imags[group].append(twos)
+                    imags[group].append(jnp.where(lane == 0, 0.0, threes))
                 else:
-                    out[a, rows, t * W : (t + 1) * W] = fold([s[0] + s[1] for s in sums])
-                    threes = fold([s[2] for s in sums])
-                    imags.append((None, threes))
+                    reals[group].append(fold([s[0] + s[1] for s in sums]))
+                    imags[group].append(threes)
         for group in range(2):
-            rows = pl.ds(group * 8, 8)
-            before = imags[group][0]
-            for t in range(4):
-                turned = pltpu.roll(imags[2 * t + group][1], 1, 1)
-                out[a, rows, (4 + t) * W : (5 + t) * W] = jnp.where(lane == 0, before, turned)
-                before = turned
-            out[a, rows, 8 * W : 8 * W + 2] = jnp.where(lane == 0, before, 0.0)[:, :2]
+            emit(a, group, reals[group], imags[group])
+
+
+def cross_kernel(off_hbm, data, part_hbm, table, out, off_ref, gate_vals, spectra, part, sem):
+    z, wp, zh, y = place()
+    load_off = pltpu.make_async_copy(off_hbm, off_ref, sem.at[0])
+    load_off.start()
+    load_part = pltpu.make_async_copy(part_hbm, part, sem.at[1])
+    load_part.start()
+    lane = lax.broadcasted_iota(jnp.int32, (8, W), 1)
+    make_spectra(data, table, gate_vals, spectra, y)
+
+    def finish(a, group, reals, imags):
+        rows = pl.ds(group * 8, 8)
+        for t in range(4):
+            out[a, rows, t * W : (t + 1) * W] = reals[t] + part[a, t, rows]
+        imags = [imags[t] + part[a, 4 + t, rows] for t in range(5)]
+        before = imags[0]
+        for t in range(4):
+            turned = pltpu.roll(imags[1 + t], 1, 1)
+            out[a, rows, (4 + t) * W : (5 + t) * W] = jnp.where(lane == 0, before, turned)
+            before = turned
+        out[a, rows, 8 * W : 8 * W + 2] = jnp.where(lane == 0, before, 0.0)[:, :2]
+
+    load_off.wait()
+    load_part.wait()
+    pair_sums(spectra, off_ref[zh] & 1, finish)
 
 
 def local(traces, gate_starts, section_offsets):
+    hbm = pl.BlockSpec(memory_space=pltpu.HBM)
     any_space = pl.BlockSpec(memory_space=pl.ANY)
-    vmem = pl.BlockSpec(memory_space=pltpu.VMEM)
     dma = pltpu.SemaphoreType.DMA
-    arrived = pl.pallas_call(
+    table = jnp.asarray(packed_table())
+    far, part = pl.pallas_call(
         gather_kernel,
-        out_shape=jax.ShapeDtypeStruct((8, BLOCKS, 16, W), bf16),
-        in_specs=[any_space, any_space, any_space],
-        out_specs=any_space,
+        out_shape=(
+            jax.ShapeDtypeStruct((4, BLOCKS, 16, W), bf16),
+            jax.ShapeDtypeStruct((4, 9, PARTNERS, W), f32),
+        ),
+        in_specs=[hbm, hbm, hbm, any_space],
+        out_specs=(any_space, any_space),
         scratch_shapes=[
+            pltpu.VMEM((4, BLOCKS, 16, W), bf16),
+            pltpu.VMEM((2 * W, NT), bf16),
+            pltpu.VMEM((SLOTS, 4, 8, W), jnp.int32),
+            pltpu.VMEM((SLOTS, 4, 2, 32, W), f32),
+            pltpu.VMEM((4, 9, PARTNERS, W), f32),
             pltpu.SMEM((PLANE, 2), jnp.int32),
             pltpu.VMEM((8, RECV, NT), bf16),
             pltpu.VMEM((8, 512), jnp.int32),
@@ -414,29 +443,36 @@
             pltpu.VMEM((2, SEC_REACH, 16, W), bf16),
             pltpu.VMEM((2, SEC_OWN + 1, 16, W), bf16),
             pltpu.VMEM((SEC_OWN + 1, 16, W), bf16),
-            dma((4,)), dma((8,)), dma((8,)), dma((8,)), dma((8,)), dma((8,)), dma((8,)),
+            dma((6,)), dma((8,)), dma((8,)), dma((8,)), dma((8,)), dma((8,)), dma((8,)),
             dma((8,)), dma((8,)), dma((8,)), dma((8,)), dma, dma, dma((18,)), dma((18,)), dma((6,)),
         ],
         compiler_params=pltpu.CompilerParams(
             collective_id=0, has_side_effects=True, vmem_limit_bytes=60 * 2**20
         ),
         name="gather",
-    )(section_offsets, traces, gate_starts)
+    )(section_offsets, traces, gate_starts, table)
+    return cross_call(section_offsets, far, part, table)
+
+
+def cross_call(section_offsets, far, part, table):
+    any_space = pl.BlockSpec(memory_space=pl.ANY)
+    vmem = pl.BlockSpec(memory_space=pltpu.VMEM)
+    dma = pltpu.SemaphoreType.DMA
     return pl.pallas_call(
         cross_kernel,
         out_shape=jax.ShapeDtypeStruct((4, PARTNERS, NT + 2), f32),
-        in_specs=[any_space, vmem, vmem],
+        in_specs=[any_space, vmem, any_space, vmem],
         out_specs=vmem,
         scratch_shapes=[
             pltpu.SMEM((2,), jnp.int32),
-            pltpu.VMEM((128, NT), f32),
-            pltpu.VMEM((SLOTS, 8, 3, 8, W), f32),
-            pltpu.VMEM((SLOTS, 4, 2, 64, W), f32),
-            dma,
+            pltpu.VMEM((SLOTS, 4, 8, W), jnp.int32),
+            pltpu.VMEM((SLOTS, 4, 2, 32, W), f32),
+            pltpu.VMEM((4, 9, PARTNERS, W), f32),
+            dma((2,)),
         ],
-        compiler_params=pltpu.CompilerParams(vmem_limit_bytes=32 * 2**20),
+        compiler_params=pltpu.CompilerParams(vmem_limit_bytes=24 * 2**20),
         name="cross",
-    )(section_offsets, arrived, jnp.asarray(packed_table()))
+    )(section_offsets, far, part, table)
 
 
 def solution(mesh):

time: 45.6 us -> 44.8 us (0.982)
  the two profiles are of different devices: /device:TPU:36 before, /device:TPU:1 now
where the time goes in v4:
time: 44.8 us; the launch traced here: 44.6 us
  Pallas kernels  42.1 us (94%)
  local copies, waits for them, and re-layouts  2.54 us (6%)
    pallas_call x1, Pallas kernels, local(): pl.pallas_call(gather_kernel, out_shape=(jax.ShapeDtypeStruct((4, BLOCKS,...  37.9 us
    pallas_call x1, Pallas kernels, cross_call(): pl.pallas_call(cross_kernel, out_shape=jax.ShapeDtypeStruct((4, PARTNERS,...  4.13 us
    unnamed x8, local copies, waits for them, and re-layouts  2.54 us

profile of v4, /device:TPU:1, one launch (start us, length us, event | category | flops | bytes accessed | tf_op | source)
XLA Modules:
  0.0 44.6 jit_solution(2944324319148474146)
XLA Ops:
  0.0 0.0 copy-start
  0.0 37.9 %gather.1 = (bf16[4,13,16,128]{3,2,1,0:T(8,128)(2,1)}, f32[4,9,16,128]{3,2,1,0:T(8,128)}) custom-call(s32[2]{0:T(128)} %off_hbm.3, bf16[8,32,1024]{2,1,0:T(8,128)(2,1)} %traces_hbm.1, s32[8,2048]{1,0:T(8,128)} %gates_hbm.1, bf16[256,1024]{1,0:T(8,128)(2,1)} %constant.2.clone.table_hbm.table), custom_call_target="tpu_custom_call" | custom-call | tf_op jit(solution)/shard_map/gather/pallas_call | solution.py:418
  37.9 0.0 copy-start.3
  37.9 0.0 copy-done
  38.0 0.6 %copy-done.3 = s32[2]{0:T(128)S(1)} copy-done((s32[2]{0:T(128)S(1)}, s32[2]{0:T(128)}, u32[]{:S(2)}) %copy-start.3) | copy-done | bytes 32
  38.6 0.0 copy-start.1
  38.6 1.0 %copy-done.1 = f32[4,9,16,128]{3,2,1,0:T(8,128)S(1)} copy-done((f32[4,9,16,128]{3,2,1,0:T(8,128)S(1)}, f32[4,9,16,128]{3,2,1,0:T(8,128)}, u32[]{:S(2)}) %copy-start.1) | copy-done | bytes 294936
  39.6 0.0 copy-start.2
  39.6 0.9 %copy-done.2 = bf16[4,13,16,128]{3,2,1,0:T(8,128)(2,1)S(1)} copy-done((bf16[4,13,16,128]{3,2,1,0:T(8,128)(2,1)S(1)}, bf16[4,13,16,128]{3,2,1,0:T(8,128)(2,1)}, u32[]{:S(2)}) %copy-start.2) | copy-done | bytes 213016
  40.5 4.1 %cross.1 = f32[4,16,1026]{2,1,0:T(8,128)} custom-call(s32[2]{0:T(128)S(1)} %copy-done.3, bf16[4,13,16,128]{3,2,1,0:T(8,128)(2,1)S(1)} %copy-done.2, f32[4,9,16,128]{3,2,1,0:T(8,128)S(1)} %copy-done.1, bf16[256,1024]{1,0:T(8,128)(2,1)S(1)} %copy-done), custom_call_target="tpu_custom_call" | custom-call | tf_op jit(solution)/shard_map/cross/pallas_call | solution.py:461
Async XLA Ops:
  0.0 38.0 %copy-start = (bf16[256,1024]{1,0:T(8,128)(2,1)S(1)}, bf16[256,1024]{1,0:T(8,128)(2,1)}, u32[]{:S(2)}) copy-start(bf16[256,1024]{1,0:T(8,128)(2,1)} %constant.2.clone.table_hbm.table) | copy-start | bytes 1572868
  37.9 0.7 %copy-start.3 = (s32[2]{0:T(128)S(1)}, s32[2]{0:T(128)}, u32[]{:S(2)}) copy-start(s32[2]{0:T(128)} %off_hbm.3) | copy-start | bytes 28
  38.6 1.0 %copy-start.1 = (f32[4,9,16,128]{3,2,1,0:T(8,128)S(1)}, f32[4,9,16,128]{3,2,1,0:T(8,128)}, u32[]{:S(2)}) copy-start(f32[4,9,16,128]{3,2,1,0:T(8,128)} %get-tuple-element.8.part_hbm) | copy-start | bytes 884740
  39.6 0.9 %copy-start.2 = (bf16[4,13,16,128]{3,2,1,0:T(8,128)(2,1)S(1)}, bf16[4,13,16,128]{3,2,1,0:T(8,128)(2,1)}, u32[]{:S(2)}) copy-start(bf16[4,13,16,128]{3,2,1,0:T(8,128)(2,1)} %get-tuple-element.7.data) | copy-start | bytes 638980

commit v5 on v4

--- a/solution.py
+++ b/solution.py
@@ -62,35 +62,46 @@
     near = [(x + dx) % 4 * 2 + (core + dc) % 2 for dx, dc in steps]
     y_peers = [(y + d) % 4 for d in (1, 3, 2)]
 
-    barrier = pltpu.get_barrier_semaphore()
-
-    def greet(to_well, to_shot):
-        pl.semaphore_signal(barrier, inc=1, device_id=(to_well, to_shot), device_id_type=MESH)
-
-    for peer in near:
-        greet(z * PLANE + peer, far_shot)
-
-    @pl.when(z < 7)
-    def _():
-        for peer in near:
-            greet((z + 1) * PLANE + peer, shot)
-
-    for peer in near[1:]:
-        greet(z * PLANE + peer, shot)
-    for peer in y_peers:
-        greet(well, zh * 4 + peer)
-
+    load_traces = pltpu.make_async_copy(traces_hbm, traces, load_sem.at[3])
+    load_traces.start()
     here = pl.multiple_of(z * 256, 256)
     ahead = pl.multiple_of(jnp.minimum(z + 1, 7) * 256, 256)
     load_here = pltpu.make_async_copy(gates_hbm.at[:, pl.ds(here, 256)], gates.at[:, pl.ds(0, 256)], load_sem.at[0])
     load_ahead = pltpu.make_async_copy(gates_hbm.at[:, pl.ds(ahead, 256)], gates.at[:, pl.ds(256, 256)], load_sem.at[1])
     load_off = pltpu.make_async_copy(off_hbm, offs.at[wp], load_sem.at[2])
+    load_table = pltpu.make_async_copy(table_hbm, table, load_sem.at[4])
     load_here.start()
-    load_traces = pltpu.make_async_copy(traces_hbm, traces, load_sem.at[3])
-    load_traces.start()
+
+    barrier = pltpu.get_barrier_semaphore()
+
+    def greet(to_well, to_shot):
+        pl.semaphore_signal(barrier, inc=1, device_id=(to_well, to_shot), device_id_type=MESH)
+
+    @pl.when(z < 7)
+    def _():
+        for peer in near:
+            greet((z + 1) * PLANE + peer, shot)
+
+    for peer in near[1:]:
+        greet(z * PLANE + peer, shot)
+    for peer in y_peers:
+        greet(well, zh * 4 + peer)
+
+    def greet_far():
+        for peer in near:
+            greet(z * PLANE + peer, far_shot)
+
+    def wait_for(more):
+        @pl.when(z > 0)
+        def _():
+            pl.semaphore_wait(barrier, 18 + more)
+
+        @pl.when(z == 0)
+        def _():
+            pl.semaphore_wait(barrier, 10 + more)
+
     load_off.start()
     load_ahead.start()
-    load_table = pltpu.make_async_copy(table_hbm, table, load_sem.at[4])
     load_table.start()
 
     @pl.when(z == 7)
@@ -103,6 +114,25 @@
     load_here.wait()
     gate_cols[...] = jnp.transpose(gates[:, :256].astype(f32))
     columns = gate_cols[pl.ds(pl.multiple_of(wp * RECV, RECV), RECV), :].astype(jnp.int32)
+    load_ahead.wait()
+    load_off.wait()
+    all_gates = gates[...]
+    halves = jnp.concatenate([all_gates >> 3, all_gates & 7], axis=0).astype(f32).astype(bf16)
+    lanes = lax.broadcasted_iota(jnp.int32, (512, W), 1)
+    index = lax.broadcasted_iota(jnp.int32, (512, W), 0)
+    for h in (1, 0):
+        own = wp * RECV + (zh + h) % 2 * SEC
+        start = (own + offs[wp, (zh + h) % 2]) // 2 * 2
+        wanted = jnp.where(lanes < 32, start + lanes, own - 32 + lanes)
+        one_hot = jnp.where(index == wanted, 1.0, 0.0).astype(bf16)
+        block = jnp.dot(halves, one_hot, preferred_element_type=f32)
+        extra[h, SEC_OWN] = block.astype(bf16)
+
+    @pl.when(zh == 0)
+    def _():
+        wait_for(0)
+        greet_far()
+
     load_traces.wait()
     for s in range(8):
         data = traces[s].astype(f32)
@@ -126,20 +156,21 @@
     for i in range(2):
         for m in range(CLASSES):
             dealt[m, i] = pairs[i * CLASSES + m]
-
-    @pl.when(z > 0)
-    def _():
-        pl.semaphore_wait(barrier, 26)
-
-    @pl.when(z == 0)
-    def _():
-        pl.semaphore_wait(barrier, 18)
+    for h in (1, 0):
+        extra[h, :SEC_OWN] = unit[pl.ds((zh + h) % 2 * SEC_OWN, SEC_OWN)]
+
+    @pl.when(zh == 1)
+    def _():
+        wait_for(8)
+        greet_far()
 
     def remote(source, target, send, receive, to_well, to_shot):
         return pltpu.make_async_remote_copy(
             src_ref=source, dst_ref=target, send_sem=send, recv_sem=receive,
             device_id=(to_well, to_shot), device_id_type=MESH,
         )
+
+    e_copy = remote(extra.at[1], far_extra, e_send, e_recv, well, far_shot)
 
     mine = pl.ds(wp * 2, 2)
     mine_ahead = pl.ds(16 + wp * 2, 2)
@@ -161,30 +192,16 @@
         copy = remote(dealt.at[near[k]], held.at[mine], a_send.at[k], a_recv.at[k], to_well, shot)
         copy.start()
         a_copies.append(copy)
-    load_off.wait()
     for k in range(1, 8):
         copy = remote(offs.at[wp], offs.at[wp], o_send.at[k], o_recv.at[k], z * PLANE + near[k], shot)
         copy.start()
         o_copies.append(copy)
     held[mine] = dealt[wp]
 
-    load_ahead.wait()
-    all_gates = gates[...]
-    halves = jnp.concatenate([all_gates >> 3, all_gates & 7], axis=0).astype(f32).astype(bf16)
-    lanes = lax.broadcasted_iota(jnp.int32, (512, W), 1)
-    index = lax.broadcasted_iota(jnp.int32, (512, W), 0)
-    for h in (1, 0):
-        section = (zh + h) % 2
-        own = wp * RECV + section * SEC
-        start = (own + offs[wp, section]) // 2 * 2
-        wanted = jnp.where(lanes < 32, start + lanes, own - 32 + lanes)
-        one_hot = jnp.where(index == wanted, 1.0, 0.0).astype(bf16)
-        block = jnp.dot(halves, one_hot, preferred_element_type=f32)
-        extra[h, :SEC_OWN] = unit[pl.ds(section * SEC_OWN, SEC_OWN)]
-        extra[h, SEC_OWN] = block.astype(bf16)
-
-    e_copy = remote(extra.at[1], far_extra, e_send, e_recv, well, far_shot)
-    e_copy.start()
+    @pl.when(zh == 1)
+    def _():
+        e_copy.start()
+
     for copy in o_copies:
         copy.wait_recv()
     for copy in a_copies:
@@ -205,15 +222,26 @@
     n_copies = []
     for k in range(8):
         to_well = z * PLANE + near[k]
-        copy = remote(picked.at[1, k], far_landed.at[wp], f_send.at[k], f_recv.at[k], to_well, far_shot)
-        copy.start()
-        f_copies.append(copy)
+        f_copies.append(remote(picked.at[1, k], far_landed.at[wp], f_send.at[k], f_recv.at[k], to_well, far_shot))
+
+    @pl.when(zh == 1)
+    def _():
+        for copy in f_copies:
+            copy.start()
+
     for k in range(1, 8):
         to_well = z * PLANE + near[k]
         copy = remote(picked.at[0, k], landed.at[wp], n_send.at[k], n_recv.at[k], to_well, shot)
         copy.start()
         n_copies.append(copy)
     landed[wp] = picked[0, 0]
+
+    @pl.when(zh == 0)
+    def _():
+        pl.semaphore_wait(barrier, 8)
+        for copy in f_copies:
+            copy.start()
+        e_copy.start()
 
     own_first = wp * 16 + zh * SEC_OWN + offs[wp, zh] // 2
 
@@ -250,24 +278,25 @@
         copy.wait_recv()
     put_in_order(0, landed)
     near_copies += pass_on(0, (0,))
+
+    for copy in near_copies:
+        copy.wait()
+    load_table.wait()
+    make_spectra(near_in, table, gate_vals, spectra, y)
+
+    def keep(a, group, reals, imags):
+        rows = pl.ds(group * 8, 8)
+        for t in range(4):
+            part[a, t, rows] = reals[t]
+        for t in range(5):
+            part[a, 4 + t, rows] = imags[t]
+
     e_copy.wait_recv()
     far_copies = pass_on(1, (1, 2))
     for copy in f_copies:
         copy.wait_recv()
     put_in_order(1, far_landed)
     far_copies += pass_on(1, (0,))
-
-    for copy in near_copies:
-        copy.wait()
-    load_table.wait()
-    make_spectra(near_in, table, gate_vals, spectra, y)
-
-    def keep(a, group, reals, imags):
-        rows = pl.ds(group * 8, 8)
-        for t in range(4):
-            part[a, t, rows] = reals[t]
-        for t in range(5):
-            part[a, 4 + t, rows] = imags[t]
 
     pair_sums(spectra, offs[wp, zh] % 2, keep)
     keep_part = pltpu.make_async_copy(part, part_hbm, load_sem.at[5])
@@ -384,12 +413,20 @@
             emit(a, group, reals[group], imags[group])
 
 
-def cross_kernel(off_hbm, data, part_hbm, table, out, off_ref, gate_vals, spectra, part, sem):
+def cross_kernel(
+    off_hbm, data_hbm, part_hbm, table_hbm, out_hbm, off_ref, data, table, gate_vals, spectra, part, out, sem, out_sem
+):
     z, wp, zh, y = place()
-    load_off = pltpu.make_async_copy(off_hbm, off_ref, sem.at[0])
+    load_data = pltpu.make_async_copy(data_hbm, data, sem.at[0])
+    load_data.start()
+    load_table = pltpu.make_async_copy(table_hbm, table, sem.at[1])
+    load_table.start()
+    load_off = pltpu.make_async_copy(off_hbm, off_ref, sem.at[2])
     load_off.start()
-    load_part = pltpu.make_async_copy(part_hbm, part, sem.at[1])
+    load_part = pltpu.make_async_copy(part_hbm, part, sem.at[3])
     load_part.start()
+    load_data.wait()
+    load_table.wait()
     lane = lax.broadcasted_iota(jnp.int32, (8, W), 1)
     make_spectra(data, table, gate_vals, spectra, y)
 
@@ -404,10 +441,14 @@
             out[a, rows, (4 + t) * W : (5 + t) * W] = jnp.where(lane == 0, before, turned)
             before = turned
         out[a, rows, 8 * W : 8 * W + 2] = jnp.where(lane == 0, before, 0.0)[:, :2]
+        if group == 1:
+            pltpu.make_async_copy(out.at[a], out_hbm.at[a], out_sem.at[a]).start()
 
     load_off.wait()
     load_part.wait()
     pair_sums(spectra, off_ref[zh] & 1, finish)
+    for a in range(4):
+        pltpu.make_async_copy(out.at[a], out_hbm.at[a], out_sem.at[a]).wait()
 
 
 def local(traces, gate_starts, section_offsets):
@@ -456,21 +497,23 @@
 
 def cross_call(section_offsets, far, part, table):
     any_space = pl.BlockSpec(memory_space=pl.ANY)
-    vmem = pl.BlockSpec(memory_space=pltpu.VMEM)
     dma = pltpu.SemaphoreType.DMA
     return pl.pallas_call(
         cross_kernel,
         out_shape=jax.ShapeDtypeStruct((4, PARTNERS, NT + 2), f32),
-        in_specs=[any_space, vmem, any_space, vmem],
-        out_specs=vmem,
+        in_specs=[any_space, any_space, any_space, any_space],
+        out_specs=any_space,
         scratch_shapes=[
             pltpu.SMEM((2,), jnp.int32),
+            pltpu.VMEM((4, BLOCKS, 16, W), bf16),
+            pltpu.VMEM((2 * W, NT), bf16),
             pltpu.VMEM((SLOTS, 4, 8, W), jnp.int32),
             pltpu.VMEM((SLOTS, 4, 2, 32, W), f32),
             pltpu.VMEM((4, 9, PARTNERS, W), f32),
-            dma((2,)),
+            pltpu.VMEM((4, PARTNERS, NT + 2), f32),
+            dma((4,)), dma((4,)),
         ],
-        compiler_params=pltpu.CompilerParams(vmem_limit_bytes=24 * 2**20),
+        compiler_params=pltpu.CompilerParams(vmem_limit_bytes=60 * 2**20),
         name="cross",
     )(section_offsets, far, part, table)
 

time: 44.8 us -> 42.6 us (0.951)
  the two profiles are of different devices: /device:TPU:1 before, /device:TPU:448 now
where the time goes in v5:
time: 42.6 us; the launch traced here: 42.4 us
  Pallas kernels  42.4 us (100%)
    pallas_call x1, Pallas kernels, local(): pl.pallas_call(gather_kernel, out_shape=(jax.ShapeDtypeStruct((4, BLOCKS,...  37.2 us
    pallas_call x1, Pallas kernels, cross_call(): pl.pallas_call(cross_kernel, out_shape=jax.ShapeDtypeStruct((4, PARTNERS,...  5.2 us

profile of v5, /device:TPU:448, one launch (start us, length us, event | category | flops | bytes accessed | tf_op | source)
XLA Modules:
  0.0 42.4 jit_solution(6709226005885954828)
XLA Ops:
  0.0 37.2 %gather.1 = (bf16[4,13,16,128]{3,2,1,0:T(8,128)(2,1)}, f32[4,9,16,128]{3,2,1,0:T(8,128)}) custom-call(s32[2]{0:T(128)} %off_hbm.3, bf16[8,32,1024]{2,1,0:T(8,128)(2,1)} %traces_hbm.1, s32[8,2048]{1,0:T(8,128)} %gates_hbm.1, bf16[256,1024]{1,0:T(8,128)(2,1)} %constant.2.clone.table_hbm), custom_call_target="tpu_custom_call" | custom-call | tf_op jit(solution)/shard_map/gather/pallas_call | solution.py:459
  37.2 5.2 %cross.1 = f32[4,16,1026]{2,1,0:T(8,128)} custom-call(s32[2]{0:T(128)} %off_hbm.3, bf16[4,13,16,128]{3,2,1,0:T(8,128)(2,1)} %get-tuple-element.7.data_hbm, f32[4,9,16,128]{3,2,1,0:T(8,128)} %get-tuple-element.8.part_hbm, bf16[256,1024]{1,0:T(8,128)(2,1)} %constant.2.clone.table_hbm), custom_call_target="tpu_custom_call" | custom-call | tf_op jit(solution)/shard_map/cross/pallas_call | solution.py:501

commit v6 on v5

--- a/solution.py
+++ b/solution.py
@@ -133,7 +133,24 @@
         wait_for(0)
         greet_far()
 
+    def remote(source, target, send, receive, to_well, to_shot):
+        return pltpu.make_async_remote_copy(
+            src_ref=source, dst_ref=target, send_sem=send, recv_sem=receive,
+            device_id=(to_well, to_shot), device_id_type=MESH,
+        )
+
     load_traces.wait()
+
+    @pl.when(zh == 1)
+    def _():
+        wait_for(8)
+        greet_far()
+
+    o_copies = []
+    for k in range(1, 8):
+        copy = remote(offs.at[wp], offs.at[wp], o_send.at[k], o_recv.at[k], z * PLANE + near[k], shot)
+        copy.start()
+        o_copies.append(copy)
     for s in range(8):
         data = traces[s].astype(f32)
         gate = jnp.broadcast_to(columns[:, s : s + 1], (RECV, W))
@@ -159,17 +176,6 @@
     for h in (1, 0):
         extra[h, :SEC_OWN] = unit[pl.ds((zh + h) % 2 * SEC_OWN, SEC_OWN)]
 
-    @pl.when(zh == 1)
-    def _():
-        wait_for(8)
-        greet_far()
-
-    def remote(source, target, send, receive, to_well, to_shot):
-        return pltpu.make_async_remote_copy(
-            src_ref=source, dst_ref=target, send_sem=send, recv_sem=receive,
-            device_id=(to_well, to_shot), device_id_type=MESH,
-        )
-
     e_copy = remote(extra.at[1], far_extra, e_send, e_recv, well, far_shot)
 
     mine = pl.ds(wp * 2, 2)
@@ -182,20 +188,15 @@
 
     @pl.when(z > 0)
     def _():
-        for k in range(8):
+        for k in (7, 6, 5, 4, 3, 2, 1, 0):
             z_copy(k).start()
 
     a_copies = []
-    o_copies = []
-    for k in range(1, 8):
+    for k in (7, 6, 5, 4, 3, 2, 1):
         to_well = z * PLANE + near[k]
         copy = remote(dealt.at[near[k]], held.at[mine], a_send.at[k], a_recv.at[k], to_well, shot)
         copy.start()
         a_copies.append(copy)
-    for k in range(1, 8):
-        copy = remote(offs.at[wp], offs.at[wp], o_send.at[k], o_recv.at[k], z * PLANE + near[k], shot)
-        copy.start()
-        o_copies.append(copy)
     held[mine] = dealt[wp]
 
     @pl.when(zh == 1)
@@ -212,24 +213,27 @@
         for k in range(8):
             z_copy(k).wait_recv()
 
-    for h in (1, 0):
+    def pick(h):
         section = (zh + h) % 2
         for k in range(8):
             first = near[k] * 16 + section * SEC_OWN + offs[near[k], section] // 2
             at = (first + (wp + 512 - first) % CLASSES) // CLASSES
             picked[h, k] = held[pl.ds(at, 2)]
+
     f_copies = []
-    n_copies = []
-    for k in range(8):
+    for k in (7, 6, 5, 4, 3, 2, 1, 0):
         to_well = z * PLANE + near[k]
         f_copies.append(remote(picked.at[1, k], far_landed.at[wp], f_send.at[k], f_recv.at[k], to_well, far_shot))
+    pick(1)
 
     @pl.when(zh == 1)
     def _():
         for copy in f_copies:
             copy.start()
 
-    for k in range(1, 8):
+    pick(0)
+    n_copies = []
+    for k in (7, 6, 5, 4, 3, 2, 1):
         to_well = z * PLANE + near[k]
         copy = remote(picked.at[0, k], landed.at[wp], n_send.at[k], n_recv.at[k], to_well, shot)
         copy.start()
@@ -246,10 +250,9 @@
     own_first = wp * 16 + zh * SEC_OWN + offs[wp, zh] // 2
 
     def pass_on(h, kinds):
-        target = (far_hbm if h else near_in).at[y]
         more = far_extra if h else extra.at[0]
 
-        def pieces(to_y):
+        def pieces(to_y, target):
             return [
                 (ordered.at[h, pl.ds(2 * to_y, REACH_PAIRS)], target.at[pl.ds(0, REACH_PAIRS)]),
                 (more.at[pl.ds(2 * to_y, OWN_PAIRS)], target.at[pl.ds(REACH_PAIRS, OWN_PAIRS)]),
@@ -260,29 +263,31 @@
         for i, peer in enumerate(y_peers):
             for kind in kinds:
                 n = (h * 3 + i) * 3 + kind
-                source, to = pieces(peer)[kind]
+                source, to = pieces(peer, far_hbm.at[i] if h else near_in.at[y])[kind]
                 copies.append(remote(source, to, y_send.at[n], y_recv.at[n], well, zh * 4 + peer))
+        kept = []
         for kind in kinds:
-            source, to = pieces(y)[kind]
-            copies.append(pltpu.make_async_copy(source, to, keep_sem.at[h * 3 + kind]))
-        for copy in copies:
+            source, to = pieces(y, near_in.at[4 if h else y])[kind]
+            kept.append(pltpu.make_async_copy(source, to, keep_sem.at[h * 3 + kind]))
+        for copy in copies + kept:
             copy.start()
-        return copies
+        return copies, kept
 
     def put_in_order(h, arrived):
         for i in range(SEC_REACH):
             ordered[h, i] = arrived[(own_first + i) % CLASSES, i // CLASSES]
 
-    near_copies = pass_on(0, (1, 2))
+    some, kept = pass_on(0, (1, 2))
     for copy in n_copies:
         copy.wait_recv()
     put_in_order(0, landed)
-    near_copies += pass_on(0, (0,))
+    more, kept_more = pass_on(0, (0,))
+    near_copies = some + kept + more + kept_more
 
     for copy in near_copies:
         copy.wait()
     load_table.wait()
-    make_spectra(near_in, table, gate_vals, spectra, y)
+    make_spectra(near_in, (0, 1, 2, 3), table, gate_vals, spectra, y)
 
     def keep(a, group, reals, imags):
         rows = pl.ds(group * 8, 8)
@@ -292,13 +297,17 @@
             part[a, 4 + t, rows] = imags[t]
 
     e_copy.wait_recv()
-    far_copies = pass_on(1, (1, 2))
+    some, kept = pass_on(1, (1, 2))
     for copy in f_copies:
         copy.wait_recv()
     put_in_order(1, far_landed)
-    far_copies += pass_on(1, (0,))
-
-    pair_sums(spectra, offs[wp, zh] % 2, keep)
+    more, kept_more = pass_on(1, (0,))
+    far_copies = some + more
+
+    for copy in kept + kept_more:
+        copy.wait()
+    make_spectra(near_in, (4,), table, gate_vals, spectra, y)
+    pair_sums(spectra, 5, offs[wp, zh] % 2, keep)
     keep_part = pltpu.make_async_copy(part, part_hbm, load_sem.at[5])
     keep_part.start()
     keep_part.wait()
@@ -333,37 +342,39 @@
     return parts[0]
 
 
-def make_spectra(data, table, gate_vals, spectra, y):
+def make_spectra(data, groups, table, gate_vals, spectra, y):
     lane = lax.broadcasted_iota(jnp.int32, (8, W), 1)
     angle = lane.astype(f32) * (2 * math.pi / W)
     cosines = jnp.cos(angle)
     sines = jnp.sin(angle)
-
-    for k in range(4):
+    pairs = {1: 6, 3: 3, 4: 2}[len(groups)]
+
+    for k in groups:
         block = pltpu.roll(data[k, BLOCKS - 1].astype(f32), (W - 4 * y) % W, 1)
         gate = (block[:8] * 8.0 + block[8:]).astype(jnp.int32)
         for slot in range(SLOTS):
             column = slot if slot < 20 else 12 + slot
             gate_vals[slot, k] = jnp.broadcast_to(gate[:, column : column + 1], (8, W))
 
-    @pl.loop(0, SLOTS // 4)
+    @pl.loop(0, SLOTS // 2 // pairs)
     def _(step):
         lefts = []
-        for p in range(2):
-            for k in range(4):
-                both = data[k, 2 * step + p].astype(f32)
+        for p in range(pairs):
+            for k in groups:
+                both = data[k, pairs * step + p].astype(f32)
                 halves = []
                 for par in range(2):
                     window = both[par * 8 : par * 8 + 8]
-                    low = jnp.where(lane >= (gate_vals[4 * step + 2 * p + par, k] & 7), window, 0.0)
+                    fine = gate_vals[2 * (pairs * step + p) + par, k] & 7
+                    low = jnp.where(lane >= fine, window, 0.0)
                     halves.append(jnp.concatenate([low, window - low], axis=1))
                 lefts.append(jnp.concatenate(halves, axis=0).astype(bf16))
         flat = jnp.dot(jnp.concatenate(lefts, axis=0), table[...], preferred_element_type=f32)
-        for p in range(2):
-            for par in range(2):
-                slot = 4 * step + 2 * p + par
-                for k in range(4):
-                    first = p * 64 + k * 16 + par * 8
+        first = 0
+        for p in range(pairs):
+            for k in groups:
+                for par in range(2):
+                    slot = 2 * (pairs * step + p) + par
                     index = ((gate_vals[slot, k] >> 3) * lane) & 127
                     cosine = jnp.take_along_axis(cosines, index, axis=1)
                     sine = jnp.take_along_axis(sines, index, axis=1)
@@ -373,9 +384,10 @@
                         imag = flat[first : first + 8, (4 + t) * W : (5 + t) * W]
                         spectra[slot, t, 0, rows, :] = cosine * real + sine * imag
                         spectra[slot, t, 1, rows, :] = cosine * imag - sine * real
-
-
-def pair_sums(spectra, odd, emit):
+                    first += 8
+
+
+def pair_sums(spectra, groups, odd, emit):
     lane = lax.broadcasted_iota(jnp.int32, (8, W), 1)
 
     @pl.loop(0, 4)
@@ -383,13 +395,13 @@
         reals = [[], []]
         imags = [[], []]
         for t in range(4):
-            own = [[spectra[20 + a, t, c, k * 8 : k * 8 + 8, :] for c in range(2)] for k in range(4)]
+            own = [[spectra[20 + a, t, c, k * 8 : k * 8 + 8, :] for c in range(2)] for k in range(groups)]
             for group in range(2):
                 sums = []
                 for j in range(8):
                     slot = a + odd + group * 8 + j
                     one = two = three = None
-                    for k in range(4):
+                    for k in range(groups):
                         re = spectra[slot, t, 0, k * 8 : k * 8 + 8, :]
                         im = spectra[slot, t, 1, k * 8 : k * 8 + 8, :]
                         first = own[k][0] * re
@@ -428,7 +440,7 @@
     load_data.wait()
     load_table.wait()
     lane = lax.broadcasted_iota(jnp.int32, (8, W), 1)
-    make_spectra(data, table, gate_vals, spectra, y)
+    make_spectra(data, (0, 1, 2), table, gate_vals, spectra, y)
 
     def finish(a, group, reals, imags):
         rows = pl.ds(group * 8, 8)
@@ -446,7 +458,7 @@
 
     load_off.wait()
     load_part.wait()
-    pair_sums(spectra, off_ref[zh] & 1, finish)
+    pair_sums(spectra, 3, off_ref[zh] & 1, finish)
     for a in range(4):
         pltpu.make_async_copy(out.at[a], out_hbm.at[a], out_sem.at[a]).wait()
 
@@ -459,16 +471,16 @@
     far, part = pl.pallas_call(
         gather_kernel,
         out_shape=(
-            jax.ShapeDtypeStruct((4, BLOCKS, 16, W), bf16),
+            jax.ShapeDtypeStruct((3, BLOCKS, 16, W), bf16),
             jax.ShapeDtypeStruct((4, 9, PARTNERS, W), f32),
         ),
         in_specs=[hbm, hbm, hbm, any_space],
         out_specs=(any_space, any_space),
         scratch_shapes=[
-            pltpu.VMEM((4, BLOCKS, 16, W), bf16),
+            pltpu.VMEM((5, BLOCKS, 16, W), bf16),
             pltpu.VMEM((2 * W, NT), bf16),
-            pltpu.VMEM((SLOTS, 4, 8, W), jnp.int32),
-            pltpu.VMEM((SLOTS, 4, 2, 32, W), f32),
+            pltpu.VMEM((SLOTS, 5, 8, W), jnp.int32),
+            pltpu.VMEM((SLOTS, 4, 2, 40, W), f32),
             pltpu.VMEM((4, 9, PARTNERS, W), f32),
             pltpu.SMEM((PLANE, 2), jnp.int32),
             pltpu.VMEM((8, RECV, NT), bf16),
@@ -505,10 +517,10 @@
         out_specs=any_space,
         scratch_shapes=[
             pltpu.SMEM((2,), jnp.int32),
-            pltpu.VMEM((4, BLOCKS, 16, W), bf16),
+            pltpu.VMEM((3, BLOCKS, 16, W), bf16),
             pltpu.VMEM((2 * W, NT), bf16),
-            pltpu.VMEM((SLOTS, 4, 8, W), jnp.int32),
-            pltpu.VMEM((SLOTS, 4, 2, 32, W), f32),
+            pltpu.VMEM((SLOTS, 3, 8, W), jnp.int32),
+            pltpu.VMEM((SLOTS, 4, 2, 24, W), f32),
             pltpu.VMEM((4, 9, PARTNERS, W), f32),
             pltpu.VMEM((4, PARTNERS, NT + 2), f32),
             dma((4,)), dma((4,)),

time: 42.6 us -> 40.9 us (0.960)
  the two profiles are of different devices: /device:TPU:448 before, /device:TPU:160 now
where the time goes in v6:
time: 40.9 us; the launch traced here: 40.8 us
  Pallas kernels  40.8 us (100%)
    pallas_call x1, Pallas kernels, local(): pl.pallas_call(gather_kernel, out_shape=(jax.ShapeDtypeStruct((3, BLOCKS,...  36.4 us
    pallas_call x1, Pallas kernels, cross_call(): pl.pallas_call(cross_kernel, out_shape=jax.ShapeDtypeStruct((4, PARTNERS,...  4.32 us

profile of v6, /device:TPU:160, one launch (start us, length us, event | category | flops | bytes accessed | tf_op | source)
XLA Modules:
  0.0 40.8 jit_solution(13863054750911403889)
XLA Ops:
  0.0 36.4 %gather.1 = (bf16[3,13,16,128]{3,2,1,0:T(8,128)(2,1)}, f32[4,9,16,128]{3,2,1,0:T(8,128)}) custom-call(s32[2]{0:T(128)} %off_hbm.3, bf16[8,32,1024]{2,1,0:T(8,128)(2,1)} %traces_hbm.1, s32[8,2048]{1,0:T(8,128)} %gates_hbm.1, bf16[256,1024]{1,0:T(8,128)(2,1)} %constant.2.clone.table_hbm), custom_call_target="tpu_custom_call" | custom-call | tf_op jit(solution)/shard_map/gather/pallas_call | solution.py:471
  36.4 4.3 %cross.1 = f32[4,16,1026]{2,1,0:T(8,128)} custom-call(s32[2]{0:T(128)} %off_hbm.3, bf16[3,13,16,128]{3,2,1,0:T(8,128)(2,1)} %get-tuple-element.7.data_hbm, f32[4,9,16,128]{3,2,1,0:T(8,128)} %get-tuple-element.8.part_hbm, bf16[256,1024]{1,0:T(8,128)(2,1)} %constant.2.clone.table_hbm), custom_call_target="tpu_custom_call" | custom-call | tf_op jit(solution)/shard_map/cross/pallas_call | solution.py:513

commit v7 on v6

--- a/solution.py
+++ b/solution.py
@@ -49,7 +49,7 @@
     near_in, table, gate_vals, spectra, part,
     offs, traces, gates, gate_cols, rows, unit, dealt, held, picked, landed, far_landed, ordered, extra, far_extra,
     load_sem, o_send, o_recv, a_send, a_recv, z_send, z_recv, n_send, n_recv,
-    f_send, f_recv, e_send, e_recv, y_send, y_recv, keep_sem,
+    f_send, f_recv, e_send, e_recv, y_send, y_recv, keep_sem, answered,
 ):
     z, wp, zh, y = place()
     x, core = wp // 2, wp % 2
@@ -87,7 +87,8 @@
     for peer in y_peers:
         greet(well, zh * 4 + peer)
 
-    def greet_far():
+    @pl.when(zh == 0)
+    def _():
         for peer in near:
             greet(z * PLANE + peer, far_shot)
 
@@ -131,7 +132,6 @@
     @pl.when(zh == 0)
     def _():
         wait_for(0)
-        greet_far()
 
     def remote(source, target, send, receive, to_well, to_shot):
         return pltpu.make_async_remote_copy(
@@ -144,7 +144,8 @@
     @pl.when(zh == 1)
     def _():
         wait_for(8)
-        greet_far()
+        for peer in near:
+            pl.semaphore_signal(answered, inc=1, device_id=(z * PLANE + peer, far_shot), device_id_type=MESH)
 
     o_copies = []
     for k in range(1, 8):
@@ -242,7 +243,7 @@
 
     @pl.when(zh == 0)
     def _():
-        pl.semaphore_wait(barrier, 8)
+        pl.semaphore_wait(answered, 8)
         for copy in f_copies:
             copy.start()
         e_copy.start()
@@ -498,6 +499,7 @@
             pltpu.VMEM((SEC_OWN + 1, 16, W), bf16),
             dma((6,)), dma((8,)), dma((8,)), dma((8,)), dma((8,)), dma((8,)), dma((8,)),
             dma((8,)), dma((8,)), dma((8,)), dma((8,)), dma, dma, dma((18,)), dma((18,)), dma((6,)),
+            pltpu.SemaphoreType.REGULAR,
         ],
         compiler_params=pltpu.CompilerParams(
             collective_id=0, has_side_effects=True, vmem_limit_bytes=60 * 2**20

time: 40.9 us -> 40.1 us (0.980)
  the two profiles are of different devices: /device:TPU:160 before, /device:TPU:32 now
where the time goes in v7:
time: 40.1 us; the launch traced here: 39.9 us
  Pallas kernels  39.9 us (100%)
    pallas_call x1, Pallas kernels, local(): pl.pallas_call(gather_kernel, out_shape=(jax.ShapeDtypeStruct((3, BLOCKS,...  35.6 us
    pallas_call x1, Pallas kernels, cross_call(): pl.pallas_call(cross_kernel, out_shape=jax.ShapeDtypeStruct((4, PARTNERS,...  4.32 us

profile of v7, /device:TPU:32, one launch (start us, length us, event | category | flops | bytes accessed | tf_op | source)
XLA Modules:
  0.0 39.9 jit_solution(7845333826408133957)
XLA Ops:
  0.0 35.6 %gather.1 = (bf16[3,13,16,128]{3,2,1,0:T(8,128)(2,1)}, f32[4,9,16,128]{3,2,1,0:T(8,128)}) custom-call(s32[2]{0:T(128)} %off_hbm.3, bf16[8,32,1024]{2,1,0:T(8,128)(2,1)} %traces_hbm.1, s32[8,2048]{1,0:T(8,128)} %gates_hbm.1, bf16[256,1024]{1,0:T(8,128)(2,1)} %constant.2.clone.table_hbm), custom_call_target="tpu_custom_call" | custom-call | tf_op jit(solution)/shard_map/gather/pallas_call | solution.py:472
  35.6 4.3 %cross.1 = f32[4,16,1026]{2,1,0:T(8,128)} custom-call(s32[2]{0:T(128)} %off_hbm.3, bf16[3,13,16,128]{3,2,1,0:T(8,128)(2,1)} %get-tuple-element.7.data_hbm, f32[4,9,16,128]{3,2,1,0:T(8,128)} %get-tuple-element.8.part_hbm, bf16[256,1024]{1,0:T(8,128)(2,1)} %constant.2.clone.table_hbm), custom_call_target="tpu_custom_call" | custom-call | tf_op jit(solution)/shard_map/cross/pallas_call | solution.py:515

commit v8 on v7

--- a/solution.py
+++ b/solution.py
@@ -343,7 +343,7 @@
     return parts[0]
 
 
-def make_spectra(data, groups, table, gate_vals, spectra, y):
+def make_spectra(data, groups, table, gate_vals, spectra, y, unroll=False):
     lane = lax.broadcasted_iota(jnp.int32, (8, W), 1)
     angle = lane.astype(f32) * (2 * math.pi / W)
     cosines = jnp.cos(angle)
@@ -357,7 +357,7 @@
             column = slot if slot < 20 else 12 + slot
             gate_vals[slot, k] = jnp.broadcast_to(gate[:, column : column + 1], (8, W))
 
-    @pl.loop(0, SLOTS // 2 // pairs)
+    @pl.loop(0, SLOTS // 2 // pairs, unroll=unroll)
     def _(step):
         lefts = []
         for p in range(pairs):
@@ -441,7 +441,7 @@
     load_data.wait()
     load_table.wait()
     lane = lax.broadcasted_iota(jnp.int32, (8, W), 1)
-    make_spectra(data, (0, 1, 2), table, gate_vals, spectra, y)
+    make_spectra(data, (0, 1, 2), table, gate_vals, spectra, y, unroll=True)
 
     def finish(a, group, reals, imags):
         rows = pl.ds(group * 8, 8)

time: 40.1 us -> 39.5 us (0.985)
  Pallas kernels: 39.9 us -> 39.3 us
    pallas_call x1, Pallas kernels: 4.32 us -> 3.7 us  [cross_call(): pl.pallas_call(cross_kernel, out_shape=jax.ShapeDtypeStruct((4, PARTNERS,...]
where the time goes in v8:
time: 39.5 us; the launch traced here: 39.3 us
  Pallas kernels  39.3 us (99%)
    pallas_call x1, Pallas kernels, local(): pl.pallas_call(gather_kernel, out_shape=(jax.ShapeDtypeStruct((3, BLOCKS,...  35.6 us
    pallas_call x1, Pallas kernels, cross_call(): pl.pallas_call(cross_kernel, out_shape=jax.ShapeDtypeStruct((4, PARTNERS,...  3.7 us

profile of v8, /device:TPU:32, one launch (start us, length us, event | category | flops | bytes accessed | tf_op | source)
XLA Modules:
  0.0 39.3 jit_solution(3323261762712381176)
XLA Ops:
  0.0 35.6 %gather.1 = (bf16[3,13,16,128]{3,2,1,0:T(8,128)(2,1)}, f32[4,9,16,128]{3,2,1,0:T(8,128)}) custom-call(s32[2]{0:T(128)} %off_hbm.3, bf16[8,32,1024]{2,1,0:T(8,128)(2,1)} %traces_hbm.1, s32[8,2048]{1,0:T(8,128)} %gates_hbm.1, bf16[256,1024]{1,0:T(8,128)(2,1)} %constant.2.clone.table_hbm), custom_call_target="tpu_custom_call" | custom-call | tf_op jit(solution)/shard_map/gather/pallas_call | solution.py:472
  35.6 3.7 %cross.1 = f32[4,16,1026]{2,1,0:T(8,128)} custom-call(s32[2]{0:T(128)} %off_hbm.3, bf16[3,13,16,128]{3,2,1,0:T(8,128)(2,1)} %get-tuple-element.7.data_hbm, f32[4,9,16,128]{3,2,1,0:T(8,128)} %get-tuple-element.8.part_hbm, bf16[256,1024]{1,0:T(8,128)(2,1)} %constant.2.clone.table_hbm), custom_call_target="tpu_custom_call" | custom-call | tf_op jit(solution)/shard_map/cross/pallas_call | solution.py:515

commit v9 on v8

--- a/solution.py
+++ b/solution.py
@@ -60,7 +60,7 @@
 
     steps = [(dx, dc) for dx in (0, 1, 3, 2) for dc in (0, 1)]
     near = [(x + dx) % 4 * 2 + (core + dc) % 2 for dx, dc in steps]
-    y_peers = [(y + d) % 4 for d in (1, 3, 2)]
+    y_peers = [(y + d) % 4 for d in (2, 1, 3)]
 
     load_traces = pltpu.make_async_copy(traces_hbm, traces, load_sem.at[3])
     load_traces.start()
@@ -227,7 +227,7 @@
         f_copies.append(remote(picked.at[1, k], far_landed.at[wp], f_send.at[k], f_recv.at[k], to_well, far_shot))
     pick(1)
 
-    @pl.when(zh == 1)
+    @pl.when((zh == 1) & (z < 6))
     def _():
         for copy in f_copies:
             copy.start()
@@ -241,7 +241,7 @@
         n_copies.append(copy)
     landed[wp] = picked[0, 0]
 
-    @pl.when(zh == 0)
+    @pl.when((zh == 0) & (z >= 4))
     def _():
         pl.semaphore_wait(answered, 8)
         for copy in f_copies:
@@ -270,25 +270,42 @@
         for kind in kinds:
             source, to = pieces(y, near_in.at[4 if h else y])[kind]
             kept.append(pltpu.make_async_copy(source, to, keep_sem.at[h * 3 + kind]))
-        for copy in copies + kept:
+        return copies, kept
+
+    def start(copies):
+        for copy in copies:
             copy.start()
-        return copies, kept
 
     def put_in_order(h, arrived):
         for i in range(SEC_REACH):
             ordered[h, i] = arrived[(own_first + i) % CLASSES, i // CLASSES]
 
     some, kept = pass_on(0, (1, 2))
+    start(some + kept)
     for copy in n_copies:
         copy.wait_recv()
+
+    @pl.when((zh == 1) & (z >= 6))
+    def _():
+        for copy in f_copies:
+            copy.start()
+
     put_in_order(0, landed)
     more, kept_more = pass_on(0, (0,))
+    start(more + kept_more)
     near_copies = some + kept + more + kept_more
 
     for copy in near_copies:
         copy.wait()
     load_table.wait()
     make_spectra(near_in, (0, 1, 2, 3), table, gate_vals, spectra, y)
+
+    @pl.when((zh == 0) & (z < 4))
+    def _():
+        pl.semaphore_wait(answered, 8)
+        for copy in f_copies:
+            copy.start()
+        e_copy.start()
 
     def keep(a, group, reals, imags):
         rows = pl.ds(group * 8, 8)
@@ -297,12 +314,29 @@
         for t in range(5):
             part[a, 4 + t, rows] = imags[t]
 
-    e_copy.wait_recv()
     some, kept = pass_on(1, (1, 2))
-    for copy in f_copies:
-        copy.wait_recv()
-    put_in_order(1, far_landed)
     more, kept_more = pass_on(1, (0,))
+
+    def pass_extra():
+        e_copy.wait_recv()
+        start(some + kept)
+
+    def pass_pairs():
+        for copy in f_copies:
+            copy.wait_recv()
+        put_in_order(1, far_landed)
+        start(more + kept_more)
+
+    @pl.when(zh == 0)
+    def _():
+        pass_extra()
+        pass_pairs()
+
+    @pl.when(zh == 1)
+    def _():
+        pass_pairs()
+        pass_extra()
+
     far_copies = some + more
 
     for copy in kept + kept_more:
@@ -343,11 +377,12 @@
     return parts[0]
 
 
-def make_spectra(data, groups, table, gate_vals, spectra, y, unroll=False):
+def make_spectra(data, groups, table, gate_vals, spectra, y, unroll=False, ready=None, circle=None):
     lane = lax.broadcasted_iota(jnp.int32, (8, W), 1)
-    angle = lane.astype(f32) * (2 * math.pi / W)
-    cosines = jnp.cos(angle)
-    sines = jnp.sin(angle)
+    if circle is None:
+        angle = lane.astype(f32) * (2 * math.pi / W)
+        circle = (jnp.cos(angle), jnp.sin(angle))
+    cosines, sines = circle
     pairs = {1: 6, 3: 3, 4: 2}[len(groups)]
 
     for k in groups:
@@ -356,6 +391,9 @@
         for slot in range(SLOTS):
             column = slot if slot < 20 else 12 + slot
             gate_vals[slot, k] = jnp.broadcast_to(gate[:, column : column + 1], (8, W))
+
+    if ready is not None:
+        ready.wait()
 
     @pl.loop(0, SLOTS // 2 // pairs, unroll=unroll)
     def _(step):
@@ -438,10 +476,12 @@
     load_off.start()
     load_part = pltpu.make_async_copy(part_hbm, part, sem.at[3])
     load_part.start()
+    lane = lax.broadcasted_iota(jnp.int32, (8, W), 1)
+    angle = lane.astype(f32) * (2 * math.pi / W)
+    circle = (jnp.cos(angle), jnp.sin(angle))
     load_data.wait()
-    load_table.wait()
     lane = lax.broadcasted_iota(jnp.int32, (8, W), 1)
-    make_spectra(data, (0, 1, 2), table, gate_vals, spectra, y, unroll=True)
+    make_spectra(data, (0, 1, 2), table, gate_vals, spectra, y, unroll=True, ready=load_table, circle=circle)
 
     def finish(a, group, reals, imags):
         rows = pl.ds(group * 8, 8)

time: 39.5 us -> 39.2 us (level)
  the two profiles are of different devices: /device:TPU:32 before, /device:TPU:448 now
where the time goes in v9:
time: 39.2 us; the launch traced here: 39.1 us
  Pallas kernels  39 us (99%)
    pallas_call x1, Pallas kernels, local(): pl.pallas_call(gather_kernel, out_shape=(jax.ShapeDtypeStruct((3, BLOCKS,...  35.4 us
    pallas_call x1, Pallas kernels, cross_call(): pl.pallas_call(cross_kernel, out_shape=jax.ShapeDtypeStruct((4, PARTNERS,...  3.62 us

profile of v9, /device:TPU:448, one launch (start us, length us, event | category | flops | bytes accessed | tf_op | source)
XLA Modules:
  0.0 39.1 jit_solution(1277726654568721666)
XLA Ops:
  0.0 35.4 %gather.1 = (bf16[3,13,16,128]{3,2,1,0:T(8,128)(2,1)}, f32[4,9,16,128]{3,2,1,0:T(8,128)}) custom-call(s32[2]{0:T(128)} %off_hbm.3, bf16[8,32,1024]{2,1,0:T(8,128)(2,1)} %traces_hbm.1, s32[8,2048]{1,0:T(8,128)} %gates_hbm.1, bf16[256,1024]{1,0:T(8,128)(2,1)} %constant.2.clone.table_hbm), custom_call_target="tpu_custom_call" | custom-call | tf_op jit(solution)/shard_map/gather/pallas_call | solution.py:512
  35.4 3.6 %cross.1 = f32[4,16,1026]{2,1,0:T(8,128)} custom-call(s32[2]{0:T(128)} %off_hbm.3, bf16[3,13,16,128]{3,2,1,0:T(8,128)(2,1)} %get-tuple-element.7.data_hbm, f32[4,9,16,128]{3,2,1,0:T(8,128)} %get-tuple-element.8.part_hbm, bf16[256,1024]{1,0:T(8,128)(2,1)} %constant.2.clone.table_hbm), custom_call_target="tpu_custom_call" | custom-call | tf_op jit(solution)/shard_map/cross/pallas_call | solution.py:555

commit v10 on v9

--- a/solution.py
+++ b/solution.py
@@ -63,7 +63,6 @@
     y_peers = [(y + d) % 4 for d in (2, 1, 3)]
 
     load_traces = pltpu.make_async_copy(traces_hbm, traces, load_sem.at[3])
-    load_traces.start()
     here = pl.multiple_of(z * 256, 256)
     ahead = pl.multiple_of(jnp.minimum(z + 1, 7) * 256, 256)
     load_here = pltpu.make_async_copy(gates_hbm.at[:, pl.ds(here, 256)], gates.at[:, pl.ds(0, 256)], load_sem.at[0])
@@ -71,6 +70,9 @@
     load_off = pltpu.make_async_copy(off_hbm, offs.at[wp], load_sem.at[2])
     load_table = pltpu.make_async_copy(table_hbm, table, load_sem.at[4])
     load_here.start()
+    load_off.start()
+    load_ahead.start()
+    load_traces.start()
 
     barrier = pltpu.get_barrier_semaphore()
 
@@ -101,8 +103,6 @@
         def _():
             pl.semaphore_wait(barrier, 10 + more)
 
-    load_off.start()
-    load_ahead.start()
     load_table.start()
 
     @pl.when(z == 7)
@@ -360,19 +360,12 @@
 
 def fold(parts):
     row = lax.broadcasted_iota(jnp.int32, (8, W), 0)
-    while len(parts) > 1:
-        half = len(parts) // 2
-        upper = (row & half) == 0
+    for step in (1, 2, 4):
+        upper = (row & step) == 0
         merged = []
-        for i in range(half):
-            first, second = parts[i], parts[i + half]
-            kept = jnp.where(upper, first, second)
-            moved = jnp.where(upper, second, first)
-            if half == 4:
-                moved = pltpu.roll(moved, 4, 0)
-            else:
-                moved = jnp.where(upper, pltpu.roll(moved, 8 - half, 0), pltpu.roll(moved, half, 0))
-            merged.append(kept + moved)
+        for first, second in zip(parts[::2], parts[1::2]):
+            moved = pltpu.roll(jnp.where(upper, second, first), 8 - step, 0)
+            merged.append(jnp.where(upper, first, second) + moved)
         parts = merged
     return parts[0]
 

time: 39.2 us -> 39.2 us (level)
  no operation moved by 1% of the time
where the time goes in v10:
time: 39.2 us; the launch traced here: 39 us
  Pallas kernels  39 us (99%)
    pallas_call x1, Pallas kernels, local(): pl.pallas_call(gather_kernel, out_shape=(jax.ShapeDtypeStruct((3, BLOCKS,...  35.4 us
    pallas_call x1, Pallas kernels, cross_call(): pl.pallas_call(cross_kernel, out_shape=jax.ShapeDtypeStruct((4, PARTNERS,...  3.56 us

profile of v10, /device:TPU:448, one launch (start us, length us, event | category | flops | bytes accessed | tf_op | source)
XLA Modules:
  0.0 39.0 jit_solution(5914948083895422564)
XLA Ops:
  0.0 35.4 %gather.1 = (bf16[3,13,16,128]{3,2,1,0:T(8,128)(2,1)}, f32[4,9,16,128]{3,2,1,0:T(8,128)}) custom-call(s32[2]{0:T(128)} %off_hbm.3, bf16[8,32,1024]{2,1,0:T(8,128)(2,1)} %traces_hbm.1, s32[8,2048]{1,0:T(8,128)} %gates_hbm.1, bf16[256,1024]{1,0:T(8,128)(2,1)} %constant.2.clone.table_hbm), custom_call_target="tpu_custom_call" | custom-call | tf_op jit(solution)/shard_map/gather/pallas_call | solution.py:505
  35.4 3.6 %cross.1 = f32[4,16,1026]{2,1,0:T(8,128)} custom-call(s32[2]{0:T(128)} %off_hbm.3, bf16[3,13,16,128]{3,2,1,0:T(8,128)(2,1)} %get-tuple-element.7.data_hbm, f32[4,9,16,128]{3,2,1,0:T(8,128)} %get-tuple-element.8.part_hbm, bf16[256,1024]{1,0:T(8,128)(2,1)} %constant.2.clone.table_hbm), custom_call_target="tpu_custom_call" | custom-call | tf_op jit(solution)/shard_map/cross/pallas_call | solution.py:548

commit v11 on v10

--- a/solution.py
+++ b/solution.py
@@ -214,28 +214,34 @@
         for k in range(8):
             z_copy(k).wait_recv()
 
-    def pick(h):
+    def pick(h, k):
         section = (zh + h) % 2
-        for k in range(8):
-            first = near[k] * 16 + section * SEC_OWN + offs[near[k], section] // 2
-            at = (first + (wp + 512 - first) % CLASSES) // CLASSES
-            picked[h, k] = held[pl.ds(at, 2)]
+        first = near[k] * 16 + section * SEC_OWN + offs[near[k], section] // 2
+        at = (first + (wp + 512 - first) % CLASSES) // CLASSES
+        picked[h, k] = held[pl.ds(at, 2)]
 
     f_copies = []
     for k in (7, 6, 5, 4, 3, 2, 1, 0):
         to_well = z * PLANE + near[k]
         f_copies.append(remote(picked.at[1, k], far_landed.at[wp], f_send.at[k], f_recv.at[k], to_well, far_shot))
-    pick(1)
+
 
     @pl.when((zh == 1) & (z < 6))
     def _():
-        for copy in f_copies:
+        for copy, k in zip(f_copies, (7, 6, 5, 4, 3, 2, 1, 0)):
+            pick(1, k)
             copy.start()
 
-    pick(0)
+    @pl.when((zh == 0) | (z >= 6))
+    def _():
+        for k in range(8):
+            pick(1, k)
+
+    pick(0, 0)
     n_copies = []
     for k in (7, 6, 5, 4, 3, 2, 1):
         to_well = z * PLANE + near[k]
+        pick(0, k)
         copy = remote(picked.at[0, k], landed.at[wp], n_send.at[k], n_recv.at[k], to_well, shot)
         copy.start()
         n_copies.append(copy)

time: 39.2 us -> 39.2 us (level)
  no operation moved by 1% of the time
where the time goes in v11:
time: 39.2 us; the launch traced here: 39 us
  Pallas kernels  39 us (99%)
    pallas_call x1, Pallas kernels, local(): pl.pallas_call(gather_kernel, out_shape=(jax.ShapeDtypeStruct((3, BLOCKS,...  35.5 us
    pallas_call x1, Pallas kernels, cross_call(): pl.pallas_call(cross_kernel, out_shape=jax.ShapeDtypeStruct((4, PARTNERS,...  3.56 us

profile of v11, /device:TPU:448, one launch (start us, length us, event | category | flops | bytes accessed | tf_op | source)
XLA Modules:
  0.0 39.0 jit_solution(4726273996204777526)
XLA Ops:
  0.0 35.5 %gather.1 = (bf16[3,13,16,128]{3,2,1,0:T(8,128)(2,1)}, f32[4,9,16,128]{3,2,1,0:T(8,128)}) custom-call(s32[2]{0:T(128)} %off_hbm.3, bf16[8,32,1024]{2,1,0:T(8,128)(2,1)} %traces_hbm.1, s32[8,2048]{1,0:T(8,128)} %gates_hbm.1, bf16[256,1024]{1,0:T(8,128)(2,1)} %constant.2.clone.table_hbm), custom_call_target="tpu_custom_call" | custom-call | tf_op jit(solution)/shard_map/gather/pallas_call | solution.py:511
  35.5 3.6 %cross.1 = f32[4,16,1026]{2,1,0:T(8,128)} custom-call(s32[2]{0:T(128)} %off_hbm.3, bf16[3,13,16,128]{3,2,1,0:T(8,128)(2,1)} %get-tuple-element.7.data_hbm, f32[4,9,16,128]{3,2,1,0:T(8,128)} %get-tuple-element.8.part_hbm, bf16[256,1024]{1,0:T(8,128)(2,1)} %constant.2.clone.table_hbm), custom_call_target="tpu_custom_call" | custom-call | tf_op jit(solution)/shard_map/cross/pallas_call | solution.py:554
